TPU v7x, 256 devices: a whole 4x4x8 slice. The times are simulated.
256 devices in a mesh: batch: 32 (over y, x, core), feat: 8 (over z).
Axes of the slice: x: 4, y: 4, z: 8, core: 2. Of those that a mesh axis runs over, the one named last changes fastest.
Arguments:
- features: bfloat16 [262144, 1024], P('batch', 'feat'), may hold values from -6 to 6
- nbr_one: int32 [15, 65536], P(None, 'batch'), may hold values from 0 to 8191
- count_one: int32 [65536], P('batch'), may hold values from 1 to 15
- nbr_two: int32 [10, 16384], P(None, 'batch'), may hold values from 0 to 2047
- count_two: int32 [16384], P('batch'), may hold values from 1 to 10
- self_one: bfloat16 [1024, 512], P('feat'), may hold values from -0.1875 to 0.1875
- neigh_one: bfloat16 [1024, 512], P('feat'), may hold values from -0.1875 to 0.1875
- bias_one: float32 [512], replicated, may hold values from -3 to 3
- self_two: bfloat16 [512, 512], replicated, may hold values from -0.25 to 0.25
- neigh_two: bfloat16 [512, 512], replicated, may hold values from -0.25 to 0.25
- bias_two: float32 [512], replicated, may hold values from -3 to 3
- cotangent: bfloat16 [16384, 512], P(('batch', 'feat')), may hold values from -6 to 6
Outputs:
- grad_self_one: float32 [1024, 512], P('feat')
- grad_neigh_one: float32 [1024, 512], P('feat')
- grad_bias_one: float32 [512], replicated
- grad_self_two: float32 [512, 512], replicated
- grad_neigh_two: float32 [512, 512], replicated
- grad_bias_two: float32 [512], replicated
Inputs may be any that keep to these rules, and one draw needn't show every extreme that they name: First count_one entries of a column are the valid ones. First count_two entries of a column are the valid ones. `nbr_one`: rows inside the mini-batch's own block of 8192 input rows. `nbr_two`: rows inside the mini-batch's own block of 2048 layer one nodes.
All inputs are finite; a program needn't handle non-finite values.
Results may differ from a plain program's by a relative error of at most 0.008.
Values may be sent and summed in bfloat16 or wider, within the bound.
A program may use at most 64 MiB of HBM per device.

v0:
```python
import jax
import jax.numpy as jnp
from jax import lax
from jax.sharding import PartitionSpec as P


def count_matrix(index, count, table_rows):
    columns = lax.broadcasted_iota(jnp.int32, (1, table_rows), 1)
    total = jnp.zeros((index.shape[1], table_rows), jnp.bfloat16)
    for k in range(index.shape[0]):
        valid = (index[k][:, None] == columns) & (k < count)[:, None]
        total = total + jnp.where(valid, 1.0, 0.0).astype(jnp.bfloat16)
    return total


def neighbour_mean(table, index, count):
    rows = index.shape[1]
    block = min(512, rows)
    blocks = rows // block
    fanout = index.shape[0]

    def one_block(pieces):
        idx, cnt = pieces
        weights = count_matrix(idx, cnt, table.shape[0])
        total = jnp.dot(weights, table, preferred_element_type=jnp.float32)
        return (total / cnt[:, None].astype(jnp.float32)).astype(jnp.bfloat16)

    stacked = jnp.transpose(index.reshape(fanout, blocks, block), (1, 0, 2))
    result = lax.map(one_block, (stacked, count.reshape(blocks, block)))
    return result.reshape(rows, table.shape[1])


def spread_back(slope_two, index_two, cnt_two, self_two, neigh_two, offset, middle):
    back_one = jnp.zeros((middle, slope_two.shape[1]), jnp.float32)
    direct = jnp.dot(slope_two, self_two.T, preferred_element_type=jnp.float32)
    back_one = lax.dynamic_update_slice(back_one, direct, (offset, 0))
    spread = jnp.dot(slope_two, neigh_two.T, preferred_element_type=jnp.float32) / cnt_two[
        :, None
    ].astype(jnp.float32)
    upper = spread.astype(jnp.bfloat16)
    lower = (spread - upper.astype(jnp.float32)).astype(jnp.bfloat16)
    weights = count_matrix(index_two, cnt_two, middle)
    dims = (((0,), (0,)), ((), ()))
    added = lax.dot_general(weights, upper, dims, preferred_element_type=jnp.float32)
    added = added + lax.dot_general(weights, lower, dims, preferred_element_type=jnp.float32)
    return back_one + added


def soft_slope(back, activation):
    return (back * (1.0 - jnp.exp(-activation.astype(jnp.float32)))).astype(jnp.bfloat16)


def on_device(
    features,
    nbr_one,
    count_one,
    nbr_two,
    count_two,
    self_one,
    neigh_one,
    bias_one,
    self_two,
    neigh_two,
    bias_two,
    cotangent,
):
    groups = lax.axis_size("feat")
    member = lax.axis_index("feat")
    middle = nbr_one.shape[1]
    seeds = nbr_two.shape[1]
    own_seeds = seeds // groups
    mean_one = neighbour_mean(features, nbr_one, count_one)
    own_rows = features[:middle]
    term = jnp.dot(own_rows, self_one, preferred_element_type=jnp.float32)
    pre_own = lax.psum_scatter(
        term + jnp.dot(mean_one, neigh_one, preferred_element_type=jnp.float32),
        "feat",
        scatter_dimension=0,
        tiled=True,
    )
    act_own = jax.nn.softplus(pre_own + bias_one).astype(jnp.bfloat16)
    act_one = lax.all_gather(act_own, "feat", axis=0, tiled=True)
    seed_start = member * own_seeds
    index_mine = lax.dynamic_slice_in_dim(nbr_two, seed_start, own_seeds, 1)
    count_mine = lax.dynamic_slice_in_dim(count_two, seed_start, own_seeds, 0)
    mean_two = neighbour_mean(act_one, index_mine, count_mine)
    own_two = lax.dynamic_slice_in_dim(act_one, seed_start, own_seeds, 0)
    pre_two = jnp.dot(own_two, self_two, preferred_element_type=jnp.float32)
    pre_two = pre_two + jnp.dot(mean_two, neigh_two, preferred_element_type=jnp.float32) + bias_two
    slope_two = (cotangent.astype(jnp.float32) * jax.nn.sigmoid(pre_two)).astype(jnp.bfloat16)
    g_self_two = jnp.dot(own_two.T, slope_two, preferred_element_type=jnp.float32)
    g_neigh_two = jnp.dot(mean_two.T, slope_two, preferred_element_type=jnp.float32)
    g_bias_two = jnp.sum(slope_two.astype(jnp.float32), axis=0)
    slope_all = lax.all_gather(slope_two, "feat", axis=0, tiled=True)
    back_one = spread_back(slope_all, nbr_two, count_two, self_two, neigh_two, 0, middle)
    slope_one = soft_slope(back_one, act_one)
    g_self_one = jnp.dot(own_rows.T, slope_one, preferred_element_type=jnp.float32)
    g_neigh_one = jnp.dot(mean_one.T, slope_one, preferred_element_type=jnp.float32)
    g_bias_one = jnp.sum(slope_one.astype(jnp.float32), axis=0)
    g_self_one, g_neigh_one, g_bias_one = lax.psum((g_self_one, g_neigh_one, g_bias_one), "batch")
    g_self_two, g_neigh_two, g_bias_two = lax.psum(
        (g_self_two, g_neigh_two, g_bias_two), ("batch", "feat")
    )
    return (g_self_one, g_neigh_one, g_bias_one, g_self_two, g_neigh_two, g_bias_two)


def solution(mesh):
    in_specs = (
        P("batch", "feat"),
        P(None, "batch"),
        P("batch"),
        P(None, "batch"),
        P("batch"),
        P("feat", None),
        P("feat", None),
        P(),
        P(),
        P(),
        P(),
        P(("batch", "feat"), None),
    )
    out_specs = (P("feat", None), P("feat", None), P(), P(), P(), P())
    return jax.shard_map(
        on_device, mesh=mesh, in_specs=in_specs, out_specs=out_specs, check_vma=False
    )
```

profile of v0, /device:TPU:1, one launch (start us, length us, event | category | flops | bytes accessed | tf_op | source)
XLA Modules:
  0.0 813.6 jit_solution(8937097443093381410)
XLA Ops:
  7.2 0.0 reduce-scatter.2.cloned.1.call-start
  7.2 1.1 reshape.235
  8.4 0.7 reshape.236
  9.1 3.7 fusion.99
  12.8 245.1 %while.2 = (s32[]{:T(128)}, bf16[4,512,128]{2,1,0:T(8,128)(2,1)S(1)}, s32[4,15,512]{2,0,1:T(4,128)S(1)}, s32[4,512]{1,0:T(4,128)S(1)}, bf16[8192,128]{1,0:T(8,12...) while((s32[]{:T(128)}, ...), condition=%wide.region_1.2_spmd, body=%wide.region_0.1_spmd.sunk | while | flops 1451368448 | bytes 2346417 | solution.py:29
  12.8 0.1 constant_dynamic-slice_fusion.18
  12.9 0.1 compare_reduce_fusion.16
  13.0 61.0 %fusion.180 = bf16[4,512,128]{2,1,0:T(8,128)(2,1)S(1)} fusion(bf16[4,512,128]{2,1,0:T(8,128)(2,1)S(1)} %get-tuple-element.275, s32[]{:T(128)S(6)} %copy.40, bf16[8192,128]{1,0:T(8,128)(2,1)S(1)} %get-tuple-element.299, s32[512]{0:T(512)S(1)} %bitcast.157, s32[512]{0:T(512)S(1)} %bitcast.144, s32[512]{0:T(512)S(1)} %bitcast.145, ...), kind=kOutput, calls=%fused_computation.78.clone.2 | convolution fusion | flops 1451360256 | bytes 2268676 | tf_op jit(solution)/shard_map/while/body/eval_jaxpr/dot_general | solution.py:25
  74.0 0.1 constant_dynamic-slice_fusion.18
  74.1 0.1 compare_reduce_fusion.16
  74.2 61.0 %fusion.180 = bf16[4,512,128]{2,1,0:T(8,128)(2,1)S(1)} fusion(bf16[4,512,128]{2,1,0:T(8,128)(2,1)S(1)} %get-tuple-element.275, s32[]{:T(128)S(6)} %copy.40, bf16[8192,128]{1,0:T(8,128)(2,1)S(1)} %get-tuple-element.299, s32[512]{0:T(512)S(1)} %bitcast.157, s32[512]{0:T(512)S(1)} %bitcast.144, s32[512]{0:T(512)S(1)} %bitcast.145, ...), kind=kOutput, calls=%fused_computation.78.clone.2 | convolution fusion | flops 1451360256 | bytes 2268676 | tf_op jit(solution)/shard_map/while/body/eval_jaxpr/dot_general | solution.py:25
  135.3 0.1 constant_dynamic-slice_fusion.18
  135.4 0.1 compare_reduce_fusion.16
  135.5 61.0 %fusion.180 = bf16[4,512,128]{2,1,0:T(8,128)(2,1)S(1)} fusion(bf16[4,512,128]{2,1,0:T(8,128)(2,1)S(1)} %get-tuple-element.275, s32[]{:T(128)S(6)} %copy.40, bf16[8192,128]{1,0:T(8,128)(2,1)S(1)} %get-tuple-element.299, s32[512]{0:T(512)S(1)} %bitcast.157, s32[512]{0:T(512)S(1)} %bitcast.144, s32[512]{0:T(512)S(1)} %bitcast.145, ...), kind=kOutput, calls=%fused_computation.78.clone.2 | convolution fusion | flops 1451360256 | bytes 2268676 | tf_op jit(solution)/shard_map/while/body/eval_jaxpr/dot_general | solution.py:25
  196.6 0.1 constant_dynamic-slice_fusion.18
  196.7 0.1 compare_reduce_fusion.16
  196.8 61.0 %fusion.180 = bf16[4,512,128]{2,1,0:T(8,128)(2,1)S(1)} fusion(bf16[4,512,128]{2,1,0:T(8,128)(2,1)S(1)} %get-tuple-element.275, s32[]{:T(128)S(6)} %copy.40, bf16[8192,128]{1,0:T(8,128)(2,1)S(1)} %get-tuple-element.299, s32[512]{0:T(512)S(1)} %bitcast.157, s32[512]{0:T(512)S(1)} %bitcast.144, s32[512]{0:T(512)S(1)} %bitcast.145, ...), kind=kOutput, calls=%fused_computation.78.clone.2 | convolution fusion | flops 1451360256 | bytes 2268676 | tf_op jit(solution)/shard_map/while/body/eval_jaxpr/dot_general | solution.py:25
  257.9 4.8 convolution_add_fusion
  262.7 0.0 reduce-scatter.2.cloned.1.call-update
  262.7 0.0 all-gather.2.cloned.1.call-start
  262.7 59.2 %reduce-scatter.2.cloned.1.call-done = f32[256,512]{1,0:T(8,128)} async-done(((f32[2048,512]{1,0:T(8,128)}), f32[256,512]{1,0:T(8,128)}) %reduce-scatter.2.cloned.1.call-update) | async-done | bytes 524304 | tf_op jit(solution)/shard_map/reduce_scatter | solution.py:75
  322.0 2.0 fusion.87
  324.0 0.0 all-gather.2.cloned.1.call-update
  324.1 0.0 all-reduce.8.cloned.1.call-start
  324.1 0.1 fusion.147
  324.2 0.1 dynamic-slice_bitcast_fusion.9
  324.4 36.0 %all-gather.2.cloned.1.call-done = bf16[2048,512]{1,0:T(8,128)(2,1)} async-done(((bf16[256,512]{1,0:T(8,128)(2,1)}), bf16[2048,512]{1,0:T(8,128)(2,1)}) %all-gather.2.cloned.1.call-update) | async-done | bytes 2097168 | tf_op jit(solution)/shard_map/all_gather | solution.py:82
  360.4 1.0 fusion.138
  361.4 3.0 fusion.85
  364.4 0.3 convert_reduce_fusion.1
  364.7 20.0 %all_gather.7 = bf16[512,512]{1,0:T(8,128)(2,1)S(1)} all-gather(bf16[64,512]{1,0:T(8,128)(2,1)S(1)} %get-tuple-element.157), channel_id=1, replica_groups=mesh['batch'=32,'feat'=8] {'feat'}, dimensions={0}, use_global_device_ids=true | all-gather | bytes 589824 | tf_op jit(solution)/shard_map/all_gather | solution.py:94
  384.6 0.5 fusion.149
  385.1 0.5 convolution_divide_fusion
  385.6 10.4 %fusion.112 = f32[2048,512]{1,0:T(8,128)S(1)} fusion(f32[512,512]{1,0:T(8,128)S(1)} %convolution_divide_fusion, s32[512]{0:T(512)S(1)} %bitcast.175, s32[512]{0:T(512)S(1)} %bitcast.177, s32[512]{0:T(512)S(1)} %bitcast.161, s32[512]{0:T(512)S(1)} %bitcast.163, s32[512]{0:T(512)S(1)} %bitcast.165, s32[512]{0:T(512)S(1)} %bitcast.167, s32[512]{0:T(512)S(1)} %bitcast.169, ...), kind=kOutput, calls=%fused_computation.212 | convolution fusion | flops 1136918528 | bytes 5268480 | tf_op jit(solution)/shard_map/dot_general | solution.py:44
  396.0 12.1 %convert_reduce_fusion = (f32[512]{0:T(512)S(1)}, bf16[2048,512]{1,0:T(8,128)(2,1)S(1)}) fusion(bf16[2048,512]{1,0:T(8,128)(2,1)S(1)} %copy-done.6, f32[2048,512]{1,0:T(8,128)S(1)} %fusion.112, f32[512,512]{1,0:T(8,128)S(1)} %convolution_divide_fusion, s32[512]{0:T(512)S(1)} %bitcast.176, s32[512]{0:T(512)S(1)} %bitcast.178, s32[512]{0:T(512)S(1)} %bitcast.162, ...), kind=kOutput, calls=%fused_computation.112 | convolution fusion | flops 1147141632 | bytes 10513408 | tf_op jit(solution)/shard_map/dot_general | solution.py:45
  408.1 2.8 convolution_bitcast_fusion
  410.9 1.2 fusion.150
  412.1 0.0 all-reduce.8.cloned.1.call-update
  412.1 0.0 all-reduce.6.cloned.1.call-start
  412.1 2.1 fusion.136
  414.3 1.3 fusion.151
  415.6 84.2 %psum.47 = f32[512]{0:T(512)} all-reduce(f32[512]{0:T(512)S(1)} %get-tuple-element.156), channel_id=1, replica_groups=mesh['batch'=32,'feat'=8] {'batch','feat'}, use_global_device_ids=true, to_apply=%region_10.11 | all-reduce | flops 512 | bytes 4096 | tf_op jit(solution)/shard_map/psum | solution.py:101
  499.8 63.2 %psum.44 = f32[512]{0:T(512)} all-reduce(f32[512]{0:T(512)S(1)} %get-tuple-element.154), channel_id=1, replica_groups=mesh['batch'=32,'feat'=8] {'batch'}, use_global_device_ids=true, to_apply=%region_6.7 | all-reduce | flops 512 | bytes 4096 | tf_op jit(solution)/shard_map/psum | solution.py:100
  563.0 1.8 copy.20
  564.8 236.1 %all-reduce.6.cloned.1.call-done = (f32[512,512]{1,0:T(8,128)}, f32[512,512]{1,0:T(8,128)}) async-done(((f32[512,512]{1,0:T(8,128)}, f32[512,512]{1,0:T(8,128)}), (f32[512,512]{1,0:T(8,128)}, f32[512,512]{1,0:T(8,128)})) %all-reduce.6.cloned.1.call-update) | async-done | bytes 2097168 | tf_op jit(solution)/shard_map/psum | solution.py:101
  800.9 1.7 copy.48
  802.6 2.3 copy.49
  804.8 2.3 copy.50
  (31 shorter events, 0.2 us)
Async XLA Ops:
  7.2 357.2 %copy-start = (bf16[512,512]{1,0:T(8,128)(2,1)S(1)}, bf16[512,512]{1,0:T(8,128)(2,1)}, u32[]{:S(2)}) copy-start(bf16[512,512]{1,0:T(8,128)(2,1)} %param.23) | copy-start | bytes 1572868
  7.2 5.6 copy-start.3
  7.2 314.8 %reduce-scatter.2.cloned.1.call-start = ((), (), s32[]{:S(2)}) async-start(), calls=%async_computation.1 | async-start | bytes 4718592 | tf_op jit(solution)/shard_map/reduce_scatter | solution.py:75
  12.8 245.1 %copy-start.2 = (bf16[128,512]{1,0:T(8,128)(2,1)S(1)}, bf16[128,512]{1,0:T(8,128)(2,1)}, u32[]{:S(2)}) copy-start(bf16[128,512]{1,0:T(8,128)(2,1)} %param.20) | copy-start | bytes 393220
  262.7 59.3 %copy-start.7 = (f32[512]{0:T(512)S(1)}, f32[512]{0:T(512)}, u32[]{:S(2)}) copy-start(f32[512]{0:T(512)} %param.21) | copy-start | bytes 6148
  262.7 61.5 %copy-start.5 = (s32[512]{0:T(512)S(1)}, s32[512]{0:T(512)}, u32[]{:S(2)}) copy-start(s32[512]{0:T(512)} %param.18) | copy-start | bytes 6148
  262.7 61.6 %copy-start.4 = (s32[10,512]{1,0:T(8,128)S(1)}, s32[10,512]{1,0:T(8,128)}, u32[]{:S(2)}) copy-start(s32[10,512]{1,0:T(8,128)} %param.17) | copy-start | bytes 61444
  262.7 97.7 %copy-start.1 = (bf16[512,512]{1,0:T(8,128)(2,1)S(1)}, bf16[512,512]{1,0:T(8,128)(2,1)}, u32[]{:S(2)}) copy-start(bf16[512,512]{1,0:T(8,128)(2,1)} %param.22) | copy-start | bytes 1572868
  262.7 97.7 %all-gather.2.cloned.1.call-start = ((), (), s32[]{:S(2)}) async-start(), calls=%async_computation.2 | async-start | bytes 2359296 | tf_op jit(solution)/shard_map/all_gather | solution.py:82
  324.1 239.0 %all-reduce.8.cloned.1.call-start = ((), (), s32[]{:S(2)}) async-start(), calls=%async_computation.4 | async-start | bytes 1048576 | tf_op jit(solution)/shard_map/psum | solution.py:100
  361.4 3.0 copy-start.8
  361.4 3.0 copy-start.9
  385.6 10.4 %copy-start.6 = (bf16[2048,512]{1,0:T(8,128)(2,1)S(1)}, bf16[2048,512]{1,0:T(8,128)(2,1)}, u32[]{:S(2)}) copy-start(bf16[2048,512]{1,0:T(8,128)(2,1)} %all-gather.2.cloned.1.call-done) | copy-start | bytes 6291460
  412.1 388.8 %all-reduce.6.cloned.1.call-start = ((), (), s32[]{:S(2)}) async-start(), calls=%async_computation.3 | async-start | bytes 4194304 | tf_op jit(solution)/shard_map/psum | solution.py:101
Sparse Core Ops, SparseCore 0:
  262.8 59.1 reduce-scatter.1
  324.4 35.9 all-gather.1
  412.2 121.6 all-reduce.7
  540.9 259.9 all-reduce.5
where the time goes:
time: 815 us; the launch traced here: 814 us
  waiting for transfers between devices  331 us (41%)
  matrix products  288 us (35%)
  blocking collectives  167 us (20%)
  between operations  13.9 us (2%)
  local copies, waits for them, and re-layouts  10.3 us (1%)
    dot_general x5, matrix products, one_block(): total = jnp.dot(weights, table, preferred_element_type=jnp.float32)  247 us
    psum x1, waiting for transfers between devices, on_device(): lax.psum((g_self_two, g_neigh_two, g_bias_two), ('batch', 'feat'))  236 us
    psum x1, blocking collectives, on_device(): lax.psum((g_self_two, g_neigh_two, g_bias_two), ('batch', 'feat'))  84.2 us
    psum x1, blocking collectives, on_device(): lax.psum((g_self_one, g_neigh_one, g_bias_one), 'batch')  63.2 us
    reduce_scatter x1, waiting for transfers between devices, on_device(): lax.psum_scatter(term + jnp.dot(mean_one, neigh_one, preferred_element_ty...  59.2 us
    all_gather x1, waiting for transfers between devices, on_device(): act_one = lax.all_gather(act_own, 'feat', axis=0, tiled=True)  36 us
    all_gather x1, blocking collectives, on_device(): slope_all = lax.all_gather(slope_two, 'feat', axis=0, tiled=True)  20 us
  transfers between devices with their start and end apart: 4, of which 3 were waited for; matrix products, arithmetic and copies ran while one was open for 1% of the time, Pallas kernels for 0%

commit v1 on v0

v1 whole, which is shorter than its diff:
```python
import functools

import jax
import jax.numpy as jnp
from jax import lax
from jax.experimental import pallas as pl
from jax.experimental.pallas import tpu as pltpu
from jax.sharding import PartitionSpec as P

MESH = pl.DeviceIdType.MESH
F32 = jnp.float32
BF16 = jnp.bfloat16
VMEM = pl.BlockSpec(memory_space=pltpu.VMEM)
SMEM = pl.BlockSpec(memory_space=pltpu.SMEM)
ANY = pl.BlockSpec(memory_space=pl.ANY)

SOURCES = 8192
MIDDLE = 2048
SEEDS = 512
HID = 512
COLS = 128
FAN_ONE = 15
FAN_TWO = 10
Z = 8
OWN = 256
OWN_SEEDS = 64
REST = 192
GROUP = 32


def tree_sum(terms):
    while len(terms) > 1:
        odd = [terms[-1]] if len(terms) % 2 else []
        terms = [a + b for a, b in zip(terms[::2], terms[1::2])] + odd
    return terms[0]


def mean_kernel(index_ref, inverse_ref, features_ref, mean_ref, table, total):
    def widen(i, carry):
        rows = pl.ds(pl.multiple_of(i * 256, 256), 256)
        table[rows, :] = features_ref[rows, :].astype(F32)
        return carry

    lax.fori_loop(0, SOURCES // 256, widen, 0)
    table[pl.ds(SOURCES, 8), :] = jnp.zeros((8, COLS), F32)

    def step(g, carry):
        block, part = g // 8, g % 8
        seed_base = block * OWN_SEEDS + part * GROUP
        rest_base = SEEDS + block * REST + (part - 2) * GROUP
        base = jnp.where(part < 2, seed_base, rest_base)
        out = pl.multiple_of(g * GROUP, GROUP)
        for j in range(GROUP):
            rows = [table[pl.ds(index_ref[k, base + j], 1), :] for k in range(FAN_ONE)]
            total[pl.ds(out + j, 1), :] = tree_sum(rows) * inverse_ref[base + j]
        return carry

    lax.fori_loop(0, MIDDLE // GROUP, step, 0)

    def narrow(i, carry):
        rows = pl.ds(pl.multiple_of(i * 256, 256), 256)
        mean_ref[rows, :] = total[rows, :].astype(BF16)
        return carry

    lax.fori_loop(0, MIDDLE // 256, narrow, 0)


def mean_in_blocks(index, inverse, features):
    return pl.pallas_call(
        mean_kernel,
        name="mean_one",
        out_shape=jax.ShapeDtypeStruct((MIDDLE, COLS), BF16),
        in_specs=[SMEM, SMEM, VMEM],
        out_specs=VMEM,
        scratch_shapes=[
            pltpu.VMEM((SOURCES + 8, COLS), F32),
            pltpu.VMEM((MIDDLE, COLS), F32),
        ],
        compiler_params=pltpu.CompilerParams(vmem_limit_bytes=32 << 20),
        cost_estimate=pl.CostEstimate(flops=60_000_000_000, bytes_accessed=3_000_000, transcendentals=0),
    )(index, inverse, features)


def dot(a, b):
    return jnp.dot(a, b, preferred_element_type=F32)


def dot_tn(a, b):
    return lax.dot_general(a, b, (((0,), (0,)), ((), ())), preferred_element_type=F32)


def dot_nt(a, b):
    return lax.dot_general(a, b, (((1,), (1,)), ((), ())), preferred_element_type=F32)


N_COPIES = 200


def step_kernel(
    features,
    mean_ref,
    self_one,
    neigh_one,
    bias_one,
    self_two,
    neigh_two,
    bias_two,
    cotangent,
    index_two,
    inverse_two,
    out_one,
    out_two,
    out_bias,
    own_in,
    act_own,
    act_cols,
    weights,
    mean_send,
    mean_land,
    mean_two,
    slope_two,
    spread_send,
    spread_cols,
    direct,
    scat_send,
    scat_own,
    slope_one,
    g2_keep,
    g2_send,
    g2_core,
    g2_sum,
    g2_plane,
    g2_piece,
    g2_z,
    g2_row,
    g1_keep,
    g1_send,
    g1_core,
    g1_sum,
    g1_plane,
    g1_piece,
    g1_z,
    bias_mine,
    bias_core,
    bias_pair,
    bias_plane,
    bias_chips,
    bias_z,
    send_sem,
    recv_sem,
    local_sem,
):
    b = lax.axis_index("batch")
    z = lax.axis_index("feat")
    core = b % 2
    x = (b // 2) % 4
    y = b // 8
    half = z // 4
    col = z % 4
    chip = y * 4 + x
    other = 1 - core
    sibling = {"batch": b + 1 - 2 * core, "feat": z}
    z_peers = [(z + d) % Z for d in range(1, Z)]
    half_peers = [(col + d) % 4 for d in range(1, 4)]
    plane_peers = [((x + d % 4) % 4, (y + d // 4) % 4) for d in range(1, 16)]

    def at_z(peer):
        return {"batch": b, "feat": peer}

    def at_plane(peer):
        return {"batch": peer[1] * 8 + peer[0] * 2 + core, "feat": z}

    used = []

    def send(src, dst, device):
        number = len(used)
        used.append(number)
        copy = pltpu.make_async_remote_copy(
            src_ref=src,
            dst_ref=dst,
            send_sem=send_sem.at[number],
            recv_sem=recv_sem.at[number],
            device_id=device,
            device_id_type=MESH,
        )
        copy.start()
        return copy

    def wait(copies):
        for copy in copies:
            copy.wait()

    def lanes(number, start=0):
        return pl.ds(pl.multiple_of(start + number * 128, 128), 128)

    def rows(number, size, start=0):
        return pl.ds(pl.multiple_of(start + number * size, 16), size)

    barrier = pltpu.get_barrier_semaphore()
    everyone = [at_z(p) for p in z_peers] + [at_plane(p) for p in plane_peers] + [sibling]
    for device in everyone:
        pl.semaphore_signal(barrier, inc=1, device_id=device, device_id_type=MESH)
    own_a = pltpu.make_async_copy(
        features.at[rows(z, OWN_SEEDS), :], own_in.at[pl.ds(0, OWN_SEEDS), lanes(z)], local_sem.at[0]
    )
    own_b = pltpu.make_async_copy(
        features.at[rows(z, REST, SEEDS), :], own_in.at[pl.ds(OWN_SEEDS, REST), lanes(z)], local_sem.at[1]
    )
    own_a.start()
    own_b.start()
    own_in[:, lanes(z, 1024)] = mean_ref[rows(z, OWN), :]
    pl.semaphore_wait(barrier, len(everyone))

    pending_mean = [
        send(mean_ref.at[rows(p, OWN), :], own_in.at[:, lanes(z, 1024)], at_z(p)) for p in z_peers
    ]
    pending_own = []
    for p in z_peers:
        pending_own.append(
            send(features.at[rows(p, OWN_SEEDS), :], own_in.at[pl.ds(0, OWN_SEEDS), lanes(z)], at_z(p))
        )
        pending_own.append(
            send(
                features.at[rows(p, REST, SEEDS), :],
                own_in.at[pl.ds(OWN_SEEDS, REST), lanes(z)],
                at_z(p),
            )
        )

    def count_block(i, carry):
        spot = lax.broadcasted_iota(jnp.int32, (64, SEEDS), 0) + (i % 4) * 64
        block = half * 4 + i // 4
        node = jnp.where(spot < OWN_SEEDS, block * OWN_SEEDS + spot, SEEDS - OWN_SEEDS + block * REST + spot)
        total = jnp.zeros((64, SEEDS), F32)
        for k in range(FAN_TWO):
            total = total + jnp.where(node == index_two[k : k + 1, :], 1.0, 0.0)
        weights[rows(i, 64), :] = total.astype(BF16)
        return carry

    lax.fori_loop(0, 16, count_block, 0)

    own_a.wait()
    own_b.wait()
    wait(pending_mean)
    wait(pending_own)

    def layer_one(n, carry):
        cols = pl.ds(pl.multiple_of(n * 256, 256), 256)
        pre = dot(own_in[:, pl.ds(0, 1024)], self_one[:, cols])
        pre = pre + dot(own_in[:, pl.ds(1024, 1024)], neigh_one[:, cols]) + bias_one[:, cols]
        act_own[:, cols] = jax.nn.softplus(pre).astype(BF16)
        return carry

    lax.fori_loop(0, 2, layer_one, 0)

    pending = [
        send(act_own.at[:, lanes(p)], act_cols.at[rows(col, OWN), :], at_z(half * 4 + p)) for p in half_peers
    ]
    act_cols[rows(col, OWN), :] = act_own[:, lanes(col)]
    wait(pending)

    share = dot_tn(act_cols[...], weights[...])
    mean_send[...] = (share.T * inverse_two[...]).astype(BF16)
    pending = [send(mean_send.at[rows(p, OWN_SEEDS), :], mean_land.at[z], at_z(p)) for p in z_peers]
    mean_land[z] = mean_send[rows(z, OWN_SEEDS), :]
    pre_self = dot(act_own[pl.ds(0, OWN_SEEDS), :], self_two[...]) + bias_two[...]
    wait(pending)
    for q in range(4):
        both = mean_land[q].astype(F32) + mean_land[4 + q].astype(F32)
        mean_two[:, q * 128 : (q + 1) * 128] = both.astype(BF16)

    pre_two = pre_self + dot(mean_two[...], neigh_two[...])
    slope = cotangent[...].astype(F32) * jax.nn.sigmoid(pre_two)
    slope_two[...] = slope.astype(BF16)

    spread = dot_nt(slope_two[...], neigh_two[...])
    inverse = inverse_two[rows(z, OWN_SEEDS), :]
    for q in range(4):
        cols = slice(q * 128, (q + 1) * 128)
        spread_send[:, cols] = (spread[:, cols] * inverse).astype(BF16)
    pending = [
        send(spread_send.at[:, lanes(p % 4)], spread_cols.at[rows(z, OWN_SEEDS), :], at_z(p)) for p in z_peers
    ]
    spread_cols[rows(z, OWN_SEEDS), :] = spread_send[:, lanes(col)]

    own_two = act_own[pl.ds(0, OWN_SEEDS), :]
    keep_self = jnp.where(core == 0, 1.0, 0.0).astype(BF16)
    keep_neigh = jnp.where(core == 0, 0.0, 1.0).astype(BF16)
    mixed_send = own_two * keep_neigh + mean_two[...] * keep_self
    mixed_keep = own_two * keep_self + mean_two[...] * keep_neigh
    g2_send[...] = dot_tn(mixed_send, slope_two[...]).astype(BF16)
    pending_g2 = [send(g2_send, g2_core, sibling)]
    g2_keep[...] = dot_tn(mixed_keep, slope_two[...])

    def direct_block(n, carry):
        cols = pl.ds(pl.multiple_of(n * 256, 256), 256)
        direct[:, cols] = dot_nt(slope_two[...], self_two[cols, :])
        return carry

    lax.fori_loop(0, 2, direct_block, 0)
    bias_two_sum = jnp.sum(slope_two[...].astype(F32), axis=0, keepdims=True)
    wait(pending)

    def scatter_block(i, carry):
        block = rows(i, OWN)
        scat_send[block, :] = dot(weights[block, :], spread_cols[...]).astype(BF16)
        return carry

    lax.fori_loop(0, 4, scatter_block, 0)
    pending = [
        send(scat_send.at[rows(p, OWN), :], scat_own.at[:, lanes(col)], at_z(half * 4 + p)) for p in half_peers
    ]
    scat_own[:, lanes(col)] = scat_send[rows(col, OWN), :]
    wait(pending_g2)

    def g2_pair(i, carry):
        block = rows(i, 128)
        g2_sum[block, :] = (g2_keep[block, :] + g2_core[block, :].astype(F32)).astype(BF16)
        return carry

    lax.fori_loop(0, 4, g2_pair, 0)
    pending_g2 = [
        send(g2_sum.at[rows(p[1], 128), lanes(p[0])], g2_plane.at[chip], at_plane(p)) for p in plane_peers
    ]
    g2_plane[chip] = g2_sum[rows(y, 128), lanes(x)]
    wait(pending)

    back = scat_own[pl.ds(0, OWN_SEEDS), :].astype(F32) + direct[...]
    gate = 1.0 - jnp.exp(-act_own[pl.ds(0, OWN_SEEDS), :].astype(F32))
    slope_one[pl.ds(0, OWN_SEEDS), :] = (back * gate).astype(BF16)
    back = scat_own[pl.ds(OWN_SEEDS, REST), :].astype(F32)
    gate = 1.0 - jnp.exp(-act_own[pl.ds(OWN_SEEDS, REST), :].astype(F32))
    slope_one[pl.ds(OWN_SEEDS, REST), :] = (back * gate).astype(BF16)

    def g1_block(t, carry):
        g1_send[t] = dot_tn(own_in[:, lanes(t, other * 1024)], slope_one[...]).astype(BF16)
        return carry

    pending = []
    for part in range(2):
        lax.fori_loop(part * 4, part * 4 + 4, g1_block, 0)
        chunk = pl.ds(part * 4, 4)
        pending.append(send(g1_send.at[chunk], g1_core.at[chunk], sibling))
    bias_one_sum = jnp.sum(slope_one[...].astype(F32), axis=0, keepdims=True)
    for i in range(4):
        bias_mine[i : i + 1, :] = bias_one_sum[:, i * 128 : (i + 1) * 128]
        bias_mine[4 + i : 5 + i, :] = bias_two_sum[:, i * 128 : (i + 1) * 128]
    pending_bias = [send(bias_mine, bias_core, sibling)]

    def g1_own(t, carry):
        g1_keep[t] = dot_tn(own_in[:, lanes(t, core * 1024)], slope_one[...])
        return carry

    lax.fori_loop(0, 8, g1_own, 0)
    wait(pending_bias)
    bias_pair[...] = bias_mine[...] + bias_core[...]
    wait(pending)

    def g1_pair(t, carry):
        both = g1_keep[t] + g1_core[t].astype(F32)
        g1_sum[t] = both.astype(BF16).reshape(4, 32, HID)
        return carry

    lax.fori_loop(0, 8, g1_pair, 0)

    pending = [
        send(g1_sum.at[:, p[1], :, lanes(p[0])], g1_plane.at[chip], at_plane(p)) for p in plane_peers
    ]
    pending_bias = [send(bias_pair, bias_plane.at[chip], at_plane(p)) for p in plane_peers]
    g1_plane[chip] = g1_sum[:, y, :, lanes(x)]
    bias_plane[chip] = bias_pair[...]

    wait(pending_g2)
    total = tree_sum([g2_plane[p].astype(F32) for p in range(16)])
    g2_piece[...] = total.astype(BF16)
    pending_g2 = [send(g2_piece.at[rows(p, 16), :], g2_z.at[z], at_z(p)) for p in z_peers]
    g2_z[z] = g2_piece[rows(z, 16), :]
    wait(pending_g2)
    total = tree_sum([g2_z[p].astype(F32) for p in range(Z)])
    g2_row[rows(z, 16), :] = total.astype(BF16)
    pending_g2 = [send(g2_row.at[rows(z, 16), :], g2_row.at[rows(z, 16), :], at_z(p)) for p in z_peers]
    wait(pending_g2)

    wait(pending)

    def g1_chips(t, carry):
        total = tree_sum([g1_plane[p, t].astype(F32) for p in range(16)])
        g1_piece[t] = total.astype(BF16)
        return carry

    lax.fori_loop(0, 8, g1_chips, 0)
    pending = [send(g1_piece.at[p], g1_z.at[z], at_z(p)) for p in z_peers]
    g1_z[z] = g1_piece[z]
    pending_g2 = [
        send(g2_row, out_two.at[core, rows(y, 128), lanes(x)], at_plane(p)) for p in plane_peers
    ]
    out_two[core, rows(y, 128), lanes(x)] = g2_row[...]
    wait(pending_bias)
    bias_chips[...] = tree_sum([bias_plane[p] for p in range(16)])
    pending_bias = [send(bias_chips, bias_z.at[z], at_z(p)) for p in z_peers]
    bias_z[z] = bias_chips[...]
    wait(pending)
    total = tree_sum([g1_z[p].astype(F32) for p in range(Z)])
    out_one[core, rows(y, 32), lanes(x)] = total.astype(BF16)

    mine = out_one.at[core, rows(y, 32), lanes(x)]
    pending = [send(mine, mine, at_plane(p)) for p in plane_peers]
    wait(pending_g2)
    pending_g2 = [send(out_two.at[core], out_two.at[core], sibling)]
    wait(pending_bias)
    out_bias[...] = tree_sum([bias_z[p] for p in range(Z)])
    wait(pending)
    pending = [send(out_one.at[core], out_one.at[core], sibling)]
    wait(pending_g2)
    wait(pending)
    assert len(used) <= N_COPIES


def training_step(*operands):
    bf16 = [
        (OWN, 2 * Z * COLS),
        (OWN, HID),
        (4 * OWN, 128),
        (4 * OWN, SEEDS),
        (SEEDS, 128),
        (Z, OWN_SEEDS, 128),
        (OWN_SEEDS, HID),
        (OWN_SEEDS, HID),
        (OWN_SEEDS, HID),
        (SEEDS, 128),
        None,
        (4 * OWN, 128),
        (OWN, HID),
        (OWN, HID),
        None,
        (HID, HID),
        (HID, HID),
        (HID, HID),
        (16, 128, 128),
        (128, 128),
        (Z, 16, 128),
        (128, 128),
        None,
        (Z, 128, HID),
        (Z, 128, HID),
        (Z, 4, 32, HID),
        (16, Z, 32, 128),
        (Z, 32, 128),
        (Z, 32, 128),
    ]
    wide = iter([(OWN_SEEDS, HID), (HID, HID), (Z, 128, HID)])
    scratch = [pltpu.VMEM(s, BF16) if s else pltpu.VMEM(next(wide), F32) for s in bf16]
    tile = (8, 128)
    scratch += [pltpu.VMEM(s, F32) for s in (tile, tile, tile, (16, *tile), tile, (Z, *tile))]
    scratch += [pltpu.SemaphoreType.DMA((N_COPIES,)), pltpu.SemaphoreType.DMA((N_COPIES,))]
    scratch += [pltpu.SemaphoreType.DMA((2,))]
    return pl.pallas_call(
        step_kernel,
        name="training_step",
        out_shape=(
            jax.ShapeDtypeStruct((2, 128, HID), BF16),
            jax.ShapeDtypeStruct((2, HID, HID), BF16),
            jax.ShapeDtypeStruct(tile, F32),
        ),
        in_specs=[ANY] + [VMEM] * (len(operands) - 1),
        out_specs=(VMEM, VMEM, VMEM),
        scratch_shapes=scratch,
        compiler_params=pltpu.CompilerParams(
            collective_id=0, has_side_effects=True, vmem_limit_bytes=48 << 20
        ),
    )(*operands)


def on_device(
    features,
    nbr_one,
    count_one,
    nbr_two,
    count_two,
    self_one,
    neigh_one,
    bias_one,
    self_two,
    neigh_two,
    bias_two,
    cotangent,
):
    self_all = lax.all_gather(self_one, "feat", axis=0, tiled=True)
    neigh_all = lax.all_gather(neigh_one, "feat", axis=0, tiled=True)
    slot = lax.broadcasted_iota(jnp.int32, nbr_one.shape, 0)
    index_one = jnp.where(slot < count_one[None, :], nbr_one, SOURCES)
    mean_one = mean_in_blocks(index_one, 1.0 / count_one.astype(F32), features)
    slot = lax.broadcasted_iota(jnp.int32, nbr_two.shape, 0)
    index_two = jnp.where(slot < count_two[None, :], nbr_two, -1)
    inverse_two = jnp.broadcast_to(1.0 / count_two.astype(F32)[:, None], (SEEDS, 128))
    one, two, bias = training_step(
        features,
        mean_one,
        self_all,
        neigh_all,
        bias_one[None, :],
        self_two,
        neigh_two,
        bias_two[None, :],
        cotangent,
        index_two,
        inverse_two,
    )
    one, two = one.astype(F32), two.astype(F32)
    return one[0], one[1], bias[:4].reshape(HID), two[0], two[1], bias[4:].reshape(HID)


def solution(mesh):
    in_specs = (
        P("batch", "feat"),
        P(None, "batch"),
        P("batch"),
        P(None, "batch"),
        P("batch"),
        P("feat", None),
        P("feat", None),
        P(),
        P(),
        P(),
        P(),
        P(("batch", "feat"), None),
    )
    out_specs = (P("feat", None), P("feat", None), P(), P(), P(), P())
    return jax.shard_map(
        on_device, mesh=mesh, in_specs=in_specs, out_specs=out_specs, check_vma=False
    )
```

time: 815 us -> 195 us (0.24)
  waiting for transfers between devices: 331 us -> 39.4 us
  matrix products: 288 us -> 0 us
  blocking collectives: 167 us -> 0 us
  Pallas kernels: 0 us -> 132 us
    dot_general x17 -> x0, matrix products: 288 us -> none  [the longest x5 247 us: one_block(): total = jnp.dot(weights, table, preferred_element_type=jnp.float32)]
    psum x2 -> x0, waiting for transfers between devices: 236 us -> none  [the longest x1 236 us: on_device(): lax.psum((g_self_two, g_neigh_two, g_bias_two), ('batch', 'feat'))]
    psum x2 -> x0, blocking collectives: 147 us -> none  [the longest x1 84.2 us: on_device(): lax.psum((g_self_two, g_neigh_two, g_bias_two), ('batch', 'feat'))]
    pallas_call x0 -> x2, Pallas kernels: none -> 132 us  [the longest x1 96.1 us: training_step(): pl.pallas_call(step_kernel, name='training_step', out_shape=(jax.ShapeDty...]
    reduce_scatter x1 -> x0, waiting for transfers between devices: 59.2 us -> none  [on_device(): lax.psum_scatter(term + jnp.dot(mean_one, neigh_one, preferred_element_ty...]
    all_gather x1 -> x0, blocking collectives: 20 us -> none  [on_device(): slope_all = lax.all_gather(slope_two, 'feat', axis=0, tiled=True)]
    all_gather x1 -> x2, waiting for transfers between devices: 36 us -> 38 us  [the longest x1 38 us: on_device(): neigh_all = lax.all_gather(neigh_one, 'feat', axis=0, tiled=True)]
  transfers between devices with their start and end apart: 4 -> 2, of which waited for: 3 -> 1; matrix products, arithmetic and copies ran while one was open for 1% -> 1% of each run, Pallas kernels for 0% -> 19%
where the time goes in v1:
time: 195 us
  Pallas kernels  132 us (68%)
  waiting for transfers between devices  39.4 us (20%)
  between operations  14.2 us (7%)
  local copies, waits for them, and re-layouts  7.09 us (4%)
  other arithmetic  1.96 us (1%)
    pallas_call x1, Pallas kernels, training_step(): pl.pallas_call(step_kernel, name='training_step', out_shape=(jax.ShapeDty...  96.1 us
    all_gather x1, waiting for transfers between devices, on_device(): neigh_all = lax.all_gather(neigh_one, 'feat', axis=0, tiled=True)  38 us
    pallas_call x1, Pallas kernels, mean_in_blocks(): pl.pallas_call(mean_kernel, name='mean_one', out_shape=jax.ShapeDtypeStru...  36.1 us
    unnamed x20, local copies, waits for them, and re-layouts  4.06 us
  transfers between devices with their start and end apart: 2, of which 1 were waited for; matrix products, arithmetic and copies ran while one was open for 1% of the time, Pallas kernels for 19%

profile of v1, /device:TPU:1, one launch (start us, length us, event | category | flops | bytes accessed | tf_op | source)
XLA Modules:
  0.0 194.9 jit_solution(4704394575904944014)
XLA Ops:
  7.2 0.0 all-gather.3.cloned.1.call-start
  7.2 0.7 all-gather.3.cloned.1.call-update
  7.9 0.0 all-gather.5.cloned.1.call-start
  7.9 0.7 all-gather.5.cloned.1.call-update
  8.6 0.7 convert_divide_fusion.inverse_ref
  9.4 0.9 fusion.index_ref
  10.3 0.0 copy-start
  10.3 1.6 copy-done
  11.9 0.0 copy-start.9
  11.9 0.0 copy-start.8
  11.9 0.0 copy-start.3
  11.9 0.0 copy-start.4
  11.9 0.0 copy-start.5
  11.9 0.0 copy-start.6
  11.9 0.0 copy-start.7
  11.9 36.1 %mean_one.1.mean_ref = bf16[2048,128]{1,0:T(8,128)(2,1)S(1)} custom-call(s32[15,2048]{1,0:T(8,128)S(1)} %fusion.index_ref, f32[2048]{0:T(1024)S(1)} %convert_divide_fusion.inverse_ref, bf16[8192,128]{1,0:T(8,128)(2,1)S(1)} %copy-done), custom_call_target="tpu_custom_call" | custom-call | flops 60000002048 | bytes 3000000 | tf_op jit(solution)/shard_map/mean_one/pallas_call | solution.py:69
  48.0 0.0 copy-done.9
  48.1 0.0 copy-done.8
  48.1 0.0 all-gather.3.cloned.1.call-done.self_one
  48.1 38.0 %all-gather.5.cloned.1.call-done.neigh_one = bf16[1024,512]{1,0:T(8,128)(2,1)} async-done(((bf16[128,512]{1,0:T(8,128)(2,1)}), bf16[1024,512]{1,0:T(8,128)(2,1)}) %all-gather.5.cloned.1.call-update) | async-done | bytes 1048592 | tf_op jit(solution)/shard_map/all_gather | solution.py:489
  86.1 0.1 broadcast_in_dim.26.inverse_two
  86.2 0.0 copy-done.3
  86.2 0.0 copy-done.4
  86.3 0.0 copy-done.5
  86.3 0.0 copy-done.6
  86.3 0.0 copy-done.7
  86.3 0.0 copy-start.1
  86.3 1.2 copy-done.1
  87.5 0.0 copy-start.2
  87.5 1.2 copy-done.2
  88.7 96.1 %training_step.1 = (bf16[2,128,512]{2,1,0:T(8,128)(2,1)S(1)}, bf16[2,512,512]{2,1,0:T(8,128)(2,1)S(1)}, f32[8,128]{1,0:T(8,128)S(1)}) custom-call(bf16[8192,128]{1,0:T(8,128)(2,1)} %features.1, bf16[2048,128]{1,0:T(8,128)(2,1)S(1)} %mean_one.1.mean_ref, bf16[1024,512]{1,0:T(8,128)(2,1)S(1)} %copy-done.1, bf16[1024,512]{1,0:T(8,128)(2,1)S(1)} %copy-done.2, ...), custom_call_target="tpu_custom_call" | custom-call | tf_op jit(solution)/shard_map/training_step/pallas_call | solution.py:457
  184.8 0.3 convert_element_type.15
  185.1 1.5 slice_bitcast_fusion
  186.7 0.8 slice_bitcast_fusion.2
  187.5 0.6 slice_bitcast_fusion.4
  (3 shorter events, 0.1 us)
Async XLA Ops:
  7.2 40.9 %all-gather.3.cloned.1.call-start = ((), (), s32[]{:S(2)}) async-start(), calls=%async_computation | async-start | bytes 1179648 | tf_op jit(solution)/shard_map/all_gather | solution.py:488
  7.9 78.2 %all-gather.5.cloned.1.call-start = ((), (), s32[]{:S(2)}) async-start(), calls=%async_computation.1 | async-start | bytes 1179648 | tf_op jit(solution)/shard_map/all_gather | solution.py:489
  10.3 1.6 copy-start
  11.9 36.2 %copy-start.9 = (s32[512]{0:T(512)S(1)}, s32[512]{0:T(512)}, u32[]{:S(2)}) copy-start(s32[512]{0:T(512)} %param.16) | copy-start | bytes 6148
  11.9 36.2 %copy-start.8 = (s32[10,512]{1,0:T(8,128)S(1)}, s32[10,512]{1,0:T(8,128)}, u32[]{:S(2)}) copy-start(s32[10,512]{1,0:T(8,128)} %param.15) | copy-start | bytes 61444
  11.9 74.4 %copy-start.3 = (bf16[512,512]{1,0:T(8,128)(2,1)S(1)}, bf16[512,512]{1,0:T(8,128)(2,1)}, u32[]{:S(2)}) copy-start(bf16[512,512]{1,0:T(8,128)(2,1)} %self_two.1) | copy-start | bytes 1572868
  11.9 74.4 %copy-start.4 = (bf16[512,512]{1,0:T(8,128)(2,1)S(1)}, bf16[512,512]{1,0:T(8,128)(2,1)}, u32[]{:S(2)}) copy-start(bf16[512,512]{1,0:T(8,128)(2,1)} %neigh_two.1) | copy-start | bytes 1572868
  11.9 74.4 %copy-start.5 = (bf16[64,512]{1,0:T(8,128)(2,1)S(1)}, bf16[64,512]{1,0:T(8,128)(2,1)}, u32[]{:S(2)}) copy-start(bf16[64,512]{1,0:T(8,128)(2,1)} %cotangent.1) | copy-start | bytes 196612
  11.9 74.4 %copy-start.6 = (f32[512]{0:T(512)S(1)}, f32[512]{0:T(512)}, u32[]{:S(2)}) copy-start(f32[512]{0:T(512)} %param.19) | copy-start | bytes 6148
  11.9 74.4 %copy-start.7 = (f32[512]{0:T(512)S(1)}, f32[512]{0:T(512)}, u32[]{:S(2)}) copy-start(f32[512]{0:T(512)} %param.22) | copy-start | bytes 6148
  86.3 1.2 copy-start.1
  87.5 1.2 copy-start.2
Sparse Core Ops, SparseCore 0:
  9.8 37.4 all-gather.2
  49.0 37.0 all-gather.4

commit v2 on v1

--- a/solution.py
+++ b/solution.py
@@ -12,7 +12,6 @@
 BF16 = jnp.bfloat16
 VMEM = pl.BlockSpec(memory_space=pltpu.VMEM)
 SMEM = pl.BlockSpec(memory_space=pltpu.SMEM)
-ANY = pl.BlockSpec(memory_space=pl.ANY)
 
 SOURCES = 8192
 MIDDLE = 2048
@@ -35,52 +34,6 @@
     return terms[0]
 
 
-def mean_kernel(index_ref, inverse_ref, features_ref, mean_ref, table, total):
-    def widen(i, carry):
-        rows = pl.ds(pl.multiple_of(i * 256, 256), 256)
-        table[rows, :] = features_ref[rows, :].astype(F32)
-        return carry
-
-    lax.fori_loop(0, SOURCES // 256, widen, 0)
-    table[pl.ds(SOURCES, 8), :] = jnp.zeros((8, COLS), F32)
-
-    def step(g, carry):
-        block, part = g // 8, g % 8
-        seed_base = block * OWN_SEEDS + part * GROUP
-        rest_base = SEEDS + block * REST + (part - 2) * GROUP
-        base = jnp.where(part < 2, seed_base, rest_base)
-        out = pl.multiple_of(g * GROUP, GROUP)
-        for j in range(GROUP):
-            rows = [table[pl.ds(index_ref[k, base + j], 1), :] for k in range(FAN_ONE)]
-            total[pl.ds(out + j, 1), :] = tree_sum(rows) * inverse_ref[base + j]
-        return carry
-
-    lax.fori_loop(0, MIDDLE // GROUP, step, 0)
-
-    def narrow(i, carry):
-        rows = pl.ds(pl.multiple_of(i * 256, 256), 256)
-        mean_ref[rows, :] = total[rows, :].astype(BF16)
-        return carry
-
-    lax.fori_loop(0, MIDDLE // 256, narrow, 0)
-
-
-def mean_in_blocks(index, inverse, features):
-    return pl.pallas_call(
-        mean_kernel,
-        name="mean_one",
-        out_shape=jax.ShapeDtypeStruct((MIDDLE, COLS), BF16),
-        in_specs=[SMEM, SMEM, VMEM],
-        out_specs=VMEM,
-        scratch_shapes=[
-            pltpu.VMEM((SOURCES + 8, COLS), F32),
-            pltpu.VMEM((MIDDLE, COLS), F32),
-        ],
-        compiler_params=pltpu.CompilerParams(vmem_limit_bytes=32 << 20),
-        cost_estimate=pl.CostEstimate(flops=60_000_000_000, bytes_accessed=3_000_000, transcendentals=0),
-    )(index, inverse, features)
-
-
 def dot(a, b):
     return jnp.dot(a, b, preferred_element_type=F32)
 
@@ -97,8 +50,9 @@
 
 
 def step_kernel(
+    index_one,
+    inverse_one,
     features,
-    mean_ref,
     self_one,
     neigh_one,
     bias_one,
@@ -111,10 +65,15 @@
     out_one,
     out_two,
     out_bias,
+    table,
+    total_one,
+    mean_one,
+    weights_mine,
+    weights_one,
     own_in,
     act_own,
     act_cols,
-    weights,
+    counts,
     mean_send,
     mean_land,
     mean_two,
@@ -148,7 +107,6 @@
     bias_z,
     send_sem,
     recv_sem,
-    local_sem,
 ):
     b = lax.axis_index("batch")
     z = lax.axis_index("feat")
@@ -200,32 +158,78 @@
     everyone = [at_z(p) for p in z_peers] + [at_plane(p) for p in plane_peers] + [sibling]
     for device in everyone:
         pl.semaphore_signal(barrier, inc=1, device_id=device, device_id_type=MESH)
-    own_a = pltpu.make_async_copy(
-        features.at[rows(z, OWN_SEEDS), :], own_in.at[pl.ds(0, OWN_SEEDS), lanes(z)], local_sem.at[0]
-    )
-    own_b = pltpu.make_async_copy(
-        features.at[rows(z, REST, SEEDS), :], own_in.at[pl.ds(OWN_SEEDS, REST), lanes(z)], local_sem.at[1]
-    )
-    own_a.start()
-    own_b.start()
-    own_in[:, lanes(z, 1024)] = mean_ref[rows(z, OWN), :]
+    def widen(i, carry):
+        block = pl.ds(pl.multiple_of(i * 256, 256), 256)
+        table[block, :] = features[block, :].astype(F32)
+        return carry
+
+    lax.fori_loop(0, SOURCES // 256, widen, 0)
+    table[pl.ds(SOURCES, 8), :] = jnp.zeros((8, COLS), F32)
+    weights_mine[pl.ds(0, COLS), :] = self_one[...]
+    weights_mine[pl.ds(COLS, COLS), :] = neigh_one[...]
+    own_in[pl.ds(0, OWN_SEEDS), lanes(2 * z)] = features[rows(z, OWN_SEEDS), :]
+    own_in[pl.ds(OWN_SEEDS, REST), lanes(2 * z)] = features[rows(z, REST, SEEDS), :]
+    cols_mine = pl.ds(pl.multiple_of(core * 256, 256), 256)
+    weights_one[z, rows(chip, 16), cols_mine] = weights_mine[rows(chip, 16), cols_mine]
     pl.semaphore_wait(barrier, len(everyone))
 
-    pending_mean = [
-        send(mean_ref.at[rows(p, OWN), :], own_in.at[:, lanes(z, 1024)], at_z(p)) for p in z_peers
-    ]
+    part = weights_one.at[z, rows(chip, 16), cols_mine]
+    pending_weights = [send(weights_mine.at[rows(chip, 16), cols_mine], part, at_z(p)) for p in z_peers]
     pending_own = []
     for p in z_peers:
         pending_own.append(
-            send(features.at[rows(p, OWN_SEEDS), :], own_in.at[pl.ds(0, OWN_SEEDS), lanes(z)], at_z(p))
+            send(features.at[rows(p, OWN_SEEDS), :], own_in.at[pl.ds(0, OWN_SEEDS), lanes(2 * z)], at_z(p))
         )
         pending_own.append(
             send(
                 features.at[rows(p, REST, SEEDS), :],
-                own_in.at[pl.ds(OWN_SEEDS, REST), lanes(z)],
+                own_in.at[pl.ds(OWN_SEEDS, REST), lanes(2 * z)],
                 at_z(p),
             )
         )
+
+    for turn, d in enumerate((4, 3, 5, 2, 6, 1, 7, 0)):
+        owner = (z + d) % Z
+
+        def gather(g, carry, owner=owner):
+            seed_base = owner * OWN_SEEDS + g * GROUP
+            rest_base = SEEDS - OWN_SEEDS + owner * REST + g * GROUP
+            base = jnp.where(g < OWN_SEEDS // GROUP, seed_base, rest_base)
+            out = pl.multiple_of(g * GROUP, GROUP)
+            for j in range(GROUP):
+                terms = [table[pl.ds(index_one[base + (k * MIDDLE + j)], 1), :] for k in range(FAN_ONE)]
+                total_one[pl.ds(out + j, 1), :] = tree_sum(terms) * inverse_one[base + j]
+            return carry
+
+        lax.fori_loop(0, OWN // GROUP, gather, 0)
+        if d:
+            mean_one[turn] = total_one[...].astype(BF16)
+            pending_own.append(send(mean_one.at[turn], own_in.at[:, lanes(2 * z + 1)], at_z(owner)))
+        else:
+            own_in[:, lanes(2 * z + 1)] = total_one[...].astype(BF16)
+        if turn == 0:
+            wait(pending_weights)
+            part = weights_one.at[:, rows(chip, 16), cols_mine]
+            pending_weights = [send(part, part, at_plane(p)) for p in plane_peers]
+        if turn == 4:
+            wait(pending_weights)
+            part = weights_one.at[:, :, cols_mine]
+            pending_weights = [send(part, part, sibling)]
+    wait(pending_weights)
+    wait(pending_own)
+
+    def layer_one(n, carry):
+        cols = pl.ds(pl.multiple_of(n * 256, 256), 256)
+        pre = dot(own_in[...], weights_one[:, :, cols].reshape(2 * Z * COLS, 256)) + bias_one[:, cols]
+        act_own[:, cols] = jax.nn.softplus(pre).astype(BF16)
+        return carry
+
+    lax.fori_loop(0, 2, layer_one, 0)
+
+    pending = [
+        send(act_own.at[:, lanes(p)], act_cols.at[rows(col, OWN), :], at_z(half * 4 + p)) for p in half_peers
+    ]
+    act_cols[rows(col, OWN), :] = act_own[:, lanes(col)]
 
     def count_block(i, carry):
         spot = lax.broadcasted_iota(jnp.int32, (64, SEEDS), 0) + (i % 4) * 64
@@ -234,32 +238,13 @@
         total = jnp.zeros((64, SEEDS), F32)
         for k in range(FAN_TWO):
             total = total + jnp.where(node == index_two[k : k + 1, :], 1.0, 0.0)
-        weights[rows(i, 64), :] = total.astype(BF16)
+        counts[rows(i, 64), :] = total.astype(BF16)
         return carry
 
     lax.fori_loop(0, 16, count_block, 0)
-
-    own_a.wait()
-    own_b.wait()
-    wait(pending_mean)
-    wait(pending_own)
-
-    def layer_one(n, carry):
-        cols = pl.ds(pl.multiple_of(n * 256, 256), 256)
-        pre = dot(own_in[:, pl.ds(0, 1024)], self_one[:, cols])
-        pre = pre + dot(own_in[:, pl.ds(1024, 1024)], neigh_one[:, cols]) + bias_one[:, cols]
-        act_own[:, cols] = jax.nn.softplus(pre).astype(BF16)
-        return carry
-
-    lax.fori_loop(0, 2, layer_one, 0)
-
-    pending = [
-        send(act_own.at[:, lanes(p)], act_cols.at[rows(col, OWN), :], at_z(half * 4 + p)) for p in half_peers
-    ]
-    act_cols[rows(col, OWN), :] = act_own[:, lanes(col)]
-    wait(pending)
-
-    share = dot_tn(act_cols[...], weights[...])
+    wait(pending)
+
+    share = dot_tn(act_cols[...], counts[...])
     mean_send[...] = (share.T * inverse_two[...]).astype(BF16)
     pending = [send(mean_send.at[rows(p, OWN_SEEDS), :], mean_land.at[z], at_z(p)) for p in z_peers]
     mean_land[z] = mean_send[rows(z, OWN_SEEDS), :]
@@ -303,7 +288,7 @@
 
     def scatter_block(i, carry):
         block = rows(i, OWN)
-        scat_send[block, :] = dot(weights[block, :], spread_cols[...]).astype(BF16)
+        scat_send[block, :] = dot(counts[block, :], spread_cols[...]).astype(BF16)
         return carry
 
     lax.fori_loop(0, 4, scatter_block, 0)
@@ -333,7 +318,7 @@
     slope_one[pl.ds(OWN_SEEDS, REST), :] = (back * gate).astype(BF16)
 
     def g1_block(t, carry):
-        g1_send[t] = dot_tn(own_in[:, lanes(t, other * 1024)], slope_one[...]).astype(BF16)
+        g1_send[t] = dot_tn(own_in[:, lanes(2 * t + other)], slope_one[...]).astype(BF16)
         return carry
 
     pending = []
@@ -348,7 +333,7 @@
     pending_bias = [send(bias_mine, bias_core, sibling)]
 
     def g1_own(t, carry):
-        g1_keep[t] = dot_tn(own_in[:, lanes(t, core * 1024)], slope_one[...])
+        g1_keep[t] = dot_tn(own_in[:, lanes(2 * t + core)], slope_one[...])
         return carry
 
     lax.fori_loop(0, 8, g1_own, 0)
@@ -418,6 +403,11 @@
 
 def training_step(*operands):
     bf16 = [
+        None,
+        None,
+        (Z - 1, OWN, COLS),
+        (2 * COLS, HID),
+        (Z, 2 * COLS, HID),
         (OWN, 2 * Z * COLS),
         (OWN, HID),
         (4 * OWN, 128),
@@ -448,12 +438,11 @@
         (Z, 32, 128),
         (Z, 32, 128),
     ]
-    wide = iter([(OWN_SEEDS, HID), (HID, HID), (Z, 128, HID)])
+    wide = iter([(SOURCES + 8, COLS), (OWN, COLS), (OWN_SEEDS, HID), (HID, HID), (Z, 128, HID)])
     scratch = [pltpu.VMEM(s, BF16) if s else pltpu.VMEM(next(wide), F32) for s in bf16]
     tile = (8, 128)
     scratch += [pltpu.VMEM(s, F32) for s in (tile, tile, tile, (16, *tile), tile, (Z, *tile))]
     scratch += [pltpu.SemaphoreType.DMA((N_COPIES,)), pltpu.SemaphoreType.DMA((N_COPIES,))]
-    scratch += [pltpu.SemaphoreType.DMA((2,))]
     return pl.pallas_call(
         step_kernel,
         name="training_step",
@@ -462,7 +451,7 @@
             jax.ShapeDtypeStruct((2, HID, HID), BF16),
             jax.ShapeDtypeStruct(tile, F32),
         ),
-        in_specs=[ANY] + [VMEM] * (len(operands) - 1),
+        in_specs=[SMEM, SMEM] + [VMEM] * (len(operands) - 2),
         out_specs=(VMEM, VMEM, VMEM),
         scratch_shapes=scratch,
         compiler_params=pltpu.CompilerParams(
@@ -485,19 +474,17 @@
     bias_two,
     cotangent,
 ):
-    self_all = lax.all_gather(self_one, "feat", axis=0, tiled=True)
-    neigh_all = lax.all_gather(neigh_one, "feat", axis=0, tiled=True)
     slot = lax.broadcasted_iota(jnp.int32, nbr_one.shape, 0)
-    index_one = jnp.where(slot < count_one[None, :], nbr_one, SOURCES)
-    mean_one = mean_in_blocks(index_one, 1.0 / count_one.astype(F32), features)
+    index_one = jnp.where(slot < count_one[None, :], nbr_one, SOURCES).reshape(-1)
     slot = lax.broadcasted_iota(jnp.int32, nbr_two.shape, 0)
     index_two = jnp.where(slot < count_two[None, :], nbr_two, -1)
     inverse_two = jnp.broadcast_to(1.0 / count_two.astype(F32)[:, None], (SEEDS, 128))
     one, two, bias = training_step(
+        index_one,
+        1.0 / count_one.astype(F32),
         features,
-        mean_one,
-        self_all,
-        neigh_all,
+        self_one,
+        neigh_one,
         bias_one[None, :],
         self_two,
         neigh_two,

time: 195 us -> 122 us (0.63)
  waiting for transfers between devices: 39.4 us -> 0 us
  Pallas kernels: 132 us -> 106 us
  between operations: 14.2 us -> 0.69 us
  local copies, waits for them, and re-layouts: 7.09 us -> 10.7 us
    all_gather x2 -> x0, waiting for transfers between devices: 38 us -> none  [the longest x1 38 us: on_device(): neigh_all = lax.all_gather(neigh_one, 'feat', axis=0, tiled=True)]
    pallas_call x1 -> x0, Pallas kernels: 36.1 us -> none  [mean_in_blocks(): pl.pallas_call(mean_kernel, name='mean_one', out_shape=jax.ShapeDtypeStru...]
    pallas_call x1, Pallas kernels: 96.1 us -> 106 us  [training_step(): pl.pallas_call(step_kernel, name='training_step', out_shape=(jax.ShapeDty...]
    unnamed x20 -> x16, local copies, waits for them, and re-layouts: 4.06 us -> 7.69 us
  transfers between devices with their start and end apart: 2 -> 0, of which waited for: 1 -> 0; matrix products, arithmetic and copies ran while one was open for 1% -> 0% of each run, Pallas kernels for 19% -> 0%
where the time goes in v2:
time: 122 us; the launch traced here: 121 us
  Pallas kernels  106 us (87%)
  local copies, waits for them, and re-layouts  10.7 us (9%)
  other arithmetic  3.4 us (3%)
    pallas_call x1, Pallas kernels, training_step(): pl.pallas_call(step_kernel, name='training_step', out_shape=(jax.ShapeDty...  106 us
    unnamed x16, local copies, waits for them, and re-layouts  7.69 us

profile of v2, /device:TPU:1, one launch (start us, length us, event | category | flops | bytes accessed | tf_op | source)
XLA Modules:
  0.0 121.1 jit_solution(8085988023026437779)
XLA Ops:
  0.6 0.7 convert_divide_fusion.1
  1.3 0.1 broadcast_in_dim.26.inverse_two
  1.5 0.9 fusion
  2.4 0.8 fusion.1.index_two
  3.2 0.7 convert_divide_fusion.inverse_one
  3.9 0.0 copy-start
  3.9 1.6 %copy-done = bf16[8192,128]{1,0:T(8,128)(2,1)S(1)} copy-done((bf16[8192,128]{1,0:T(8,128)(2,1)S(1)}, bf16[8192,128]{1,0:T(8,128)(2,1)}, u32[]{:S(2)}) %copy-start) | copy-done | bytes 2097176
  5.5 0.0 copy-start.1
  5.5 1.0 copy-done.1
  6.5 0.0 copy-start.2
  6.5 1.0 copy-done.2
  7.6 0.0 copy-start.3
  7.6 0.9 copy-done.3
  8.5 0.0 copy-start.4
  8.5 0.9 copy-done.4
  9.4 0.0 copy-start.5
  9.4 0.8 copy-done.5
  10.2 0.0 copy-start.6
  10.2 0.7 copy-done.6
  10.9 0.0 copy-start.7
  10.9 0.7 copy-done.7
  11.6 106.2 %training_step.1 = (bf16[2,128,512]{2,1,0:T(8,128)(2,1)S(1)}, bf16[2,512,512]{2,1,0:T(8,128)(2,1)S(1)}, f32[8,128]{1,0:T(8,128)S(1)}) custom-call(s32[30720]{0:T(1024)S(1)} %reshape.25.index_one, f32[2048]{0:T(1024)S(1)} %convert_divide_fusion.inverse_one, bf16[8192,128]{1,0:T(8,128)(2,1)S(1)} %copy-done, bf16[128,512]{1,0:T(8,128)(2,1)S(1)} %copy-done.3, ...), custom_call_target="tpu_custom_call" | custom-call | tf_op jit(solution)/shard_map/training_step/pallas_call | solution.py:446
  117.8 0.3 convert_element_type.15
  118.1 1.5 %slice_bitcast_fusion = (f32[512,512]{1,0:T(8,128)}, f32[512,512]{1,0:T(8,128)}) fusion(f32[2,512,512]{2,1,0:T(8,128)S(1)} %convert_element_type.15), kind=kLoop, calls=%fused_computation | loop fusion | bytes 4194304 | tf_op jit(solution)/shard_map/squeeze | solution.py:497
  119.6 0.8 slice_bitcast_fusion.2
  120.5 0.6 slice_bitcast_fusion.4
  (2 shorter events, 0.1 us)
Async XLA Ops:
  3.9 1.6 %copy-start = (bf16[8192,128]{1,0:T(8,128)(2,1)S(1)}, bf16[8192,128]{1,0:T(8,128)(2,1)}, u32[]{:S(2)}) copy-start(bf16[8192,128]{1,0:T(8,128)(2,1)} %features.1) | copy-start | bytes 6291460
  5.5 1.0 copy-start.1
  6.5 1.0 copy-start.2
  7.6 0.9 copy-start.3
  8.5 0.9 copy-start.4
  9.4 0.8 copy-start.5
  10.2 0.7 copy-start.6
  10.9 0.7 copy-start.7

commit v3 on v2

--- a/solution.py
+++ b/solution.py
@@ -12,6 +12,7 @@
 BF16 = jnp.bfloat16
 VMEM = pl.BlockSpec(memory_space=pltpu.VMEM)
 SMEM = pl.BlockSpec(memory_space=pltpu.SMEM)
+HBM = pl.BlockSpec(memory_space=pltpu.HBM)
 
 SOURCES = 8192
 MIDDLE = 2048
@@ -51,20 +52,31 @@
 
 def step_kernel(
     index_one,
-    inverse_one,
-    features,
+    features_in,
+    count_one_in,
     self_one,
     neigh_one,
+    bias_one_in,
+    self_two_in,
+    neigh_two_in,
+    bias_two_in,
+    cotangent_in,
+    nbr_two_in,
+    count_two_in,
+    out_one,
+    out_two,
+    out_bias,
+    features,
+    count_one,
     bias_one,
     self_two,
     neigh_two,
     bias_two,
     cotangent,
-    index_two,
+    nbr_two,
+    count_two,
+    inverse_one,
     inverse_two,
-    out_one,
-    out_two,
-    out_bias,
     table,
     total_one,
     mean_one,
@@ -96,17 +108,25 @@
     g1_send,
     g1_core,
     g1_sum,
-    g1_plane,
+    g1_first_x,
+    g1_part_x,
+    g1_then_y,
+    g1_first_y,
+    g1_part_y,
+    g1_then_x,
     g1_piece,
     g1_z,
     bias_mine,
     bias_core,
     bias_pair,
-    bias_plane,
+    bias_x,
+    bias_row,
+    bias_y,
     bias_chips,
     bias_z,
     send_sem,
     recv_sem,
+    load_sem,
 ):
     b = lax.axis_index("batch")
     z = lax.axis_index("feat")
@@ -119,6 +139,7 @@
     other = 1 - core
     sibling = {"batch": b + 1 - 2 * core, "feat": z}
     z_peers = [(z + d) % Z for d in range(1, Z)]
+    ring_peers = lambda place: [(place + d) % 4 for d in range(1, 4)]
     half_peers = [(col + d) % 4 for d in range(1, 4)]
     plane_peers = [((x + d % 4) % 4, (y + d // 4) % 4) for d in range(1, 16)]
 
@@ -158,17 +179,46 @@
     everyone = [at_z(p) for p in z_peers] + [at_plane(p) for p in plane_peers] + [sibling]
     for device in everyone:
         pl.semaphore_signal(barrier, inc=1, device_id=device, device_id_type=MESH)
+    quarter = SOURCES // 4
+    loads = [
+        pltpu.make_async_copy(
+            features_in.at[pl.ds(i * quarter, quarter), :],
+            features.at[pl.ds(i * quarter, quarter), :],
+            load_sem.at[i],
+        )
+        for i in range(4)
+    ]
+    pairs = (
+        (self_one, weights_mine.at[pl.ds(0, COLS), :]),
+        (neigh_one, weights_mine.at[pl.ds(COLS, COLS), :]),
+        (count_one_in, count_one),
+        (bias_one_in, bias_one),
+        (self_two_in, self_two),
+        (neigh_two_in, neigh_two),
+        (bias_two_in, bias_two),
+        (cotangent_in, cotangent),
+        (nbr_two_in, nbr_two),
+        (count_two_in, count_two),
+    )
+    loads += [
+        pltpu.make_async_copy(src, dst, load_sem.at[4 + i]) for i, (src, dst) in enumerate(pairs)
+    ]
+    for load in loads:
+        load.start()
+
     def widen(i, carry):
         block = pl.ds(pl.multiple_of(i * 256, 256), 256)
         table[block, :] = features[block, :].astype(F32)
         return carry
 
-    lax.fori_loop(0, SOURCES // 256, widen, 0)
     table[pl.ds(SOURCES, 8), :] = jnp.zeros((8, COLS), F32)
-    weights_mine[pl.ds(0, COLS), :] = self_one[...]
-    weights_mine[pl.ds(COLS, COLS), :] = neigh_one[...]
+    steps = quarter // 256
+    loads[0].wait()
+    lax.fori_loop(0, steps, widen, 0)
     own_in[pl.ds(0, OWN_SEEDS), lanes(2 * z)] = features[rows(z, OWN_SEEDS), :]
     own_in[pl.ds(OWN_SEEDS, REST), lanes(2 * z)] = features[rows(z, REST, SEEDS), :]
+    for load in loads[4:]:
+        load.wait()
     cols_mine = pl.ds(pl.multiple_of(core * 256, 256), 256)
     weights_one[z, rows(chip, 16), cols_mine] = weights_mine[rows(chip, 16), cols_mine]
     pl.semaphore_wait(barrier, len(everyone))
@@ -188,6 +238,14 @@
             )
         )
 
+    for i in range(1, 4):
+        loads[i].wait()
+        lax.fori_loop(i * steps, (i + 1) * steps, widen, 0)
+
+    for i in range(MIDDLE // 128):
+        line = 1.0 / count_one[i : i + 1, :].astype(F32)
+        inverse_one[i * 128 : (i + 1) * 128, :] = jnp.broadcast_to(line, (128, 128)).T
+
     for turn, d in enumerate((4, 3, 5, 2, 6, 1, 7, 0)):
         owner = (z + d) % Z
 
@@ -198,20 +256,24 @@
             out = pl.multiple_of(g * GROUP, GROUP)
             for j in range(GROUP):
                 terms = [table[pl.ds(index_one[base + (k * MIDDLE + j)], 1), :] for k in range(FAN_ONE)]
-                total_one[pl.ds(out + j, 1), :] = tree_sum(terms) * inverse_one[base + j]
+                total_one[pl.ds(out + j, 1), :] = tree_sum(terms)
             return carry
 
         lax.fori_loop(0, OWN // GROUP, gather, 0)
+        seeds = total_one[pl.ds(0, OWN_SEEDS), :] * inverse_one[rows(owner, OWN_SEEDS), :]
+        rest = total_one[pl.ds(OWN_SEEDS, REST), :] * inverse_one[rows(owner, REST, SEEDS), :]
         if d:
-            mean_one[turn] = total_one[...].astype(BF16)
+            mean_one[turn, pl.ds(0, OWN_SEEDS), :] = seeds.astype(BF16)
+            mean_one[turn, pl.ds(OWN_SEEDS, REST), :] = rest.astype(BF16)
             pending_own.append(send(mean_one.at[turn], own_in.at[:, lanes(2 * z + 1)], at_z(owner)))
         else:
-            own_in[:, lanes(2 * z + 1)] = total_one[...].astype(BF16)
-        if turn == 0:
+            own_in[pl.ds(0, OWN_SEEDS), lanes(2 * z + 1)] = seeds.astype(BF16)
+            own_in[pl.ds(OWN_SEEDS, REST), lanes(2 * z + 1)] = rest.astype(BF16)
+        if turn == 1:
             wait(pending_weights)
             part = weights_one.at[:, rows(chip, 16), cols_mine]
             pending_weights = [send(part, part, at_plane(p)) for p in plane_peers]
-        if turn == 4:
+        if turn == 6:
             wait(pending_weights)
             part = weights_one.at[:, :, cols_mine]
             pending_weights = [send(part, part, sibling)]
@@ -230,6 +292,12 @@
         send(act_own.at[:, lanes(p)], act_cols.at[rows(col, OWN), :], at_z(half * 4 + p)) for p in half_peers
     ]
     act_cols[rows(col, OWN), :] = act_own[:, lanes(col)]
+
+    index_two = [
+        jnp.where(count_two[...] > k, nbr_two[k : k + 1, :], -1) for k in range(FAN_TWO)
+    ]
+    inverse = 1.0 / count_two[...].astype(F32)
+    inverse_two[...] = jnp.broadcast_to(inverse, (128, SEEDS)).T
 
     def count_block(i, carry):
         spot = lax.broadcasted_iota(jnp.int32, (64, SEEDS), 0) + (i % 4) * 64
@@ -237,7 +305,7 @@
         node = jnp.where(spot < OWN_SEEDS, block * OWN_SEEDS + spot, SEEDS - OWN_SEEDS + block * REST + spot)
         total = jnp.zeros((64, SEEDS), F32)
         for k in range(FAN_TWO):
-            total = total + jnp.where(node == index_two[k : k + 1, :], 1.0, 0.0)
+            total = total + jnp.where(node == index_two[k], 1.0, 0.0)
         counts[rows(i, 64), :] = total.astype(BF16)
         return carry
 
@@ -326,34 +394,35 @@
         lax.fori_loop(part * 4, part * 4 + 4, g1_block, 0)
         chunk = pl.ds(part * 4, 4)
         pending.append(send(g1_send.at[chunk], g1_core.at[chunk], sibling))
+
+    def g1_own(t, carry):
+        g1_keep[t] = dot_tn(own_in[:, lanes(2 * t + core)], slope_one[...])
+        return carry
+
+    def g1_pair(t, carry):
+        both = g1_keep[t] + g1_core[t].astype(F32)
+        g1_sum[t] = both.astype(BF16).reshape(4, 32, HID)
+        return carry
+
+    lax.fori_loop(0, 4, g1_own, 0)
+    wait(pending[:1])
+    lax.fori_loop(0, 4, g1_pair, 0)
+    low, high = pl.ds(0, 4), pl.ds(4, 4)
+    pending_x = [
+        send(g1_sum.at[low, :, :, lanes(p)], g1_first_x.at[x], at_plane((p, y))) for p in ring_peers(x)
+    ]
+    g1_first_x[x] = g1_sum[0:4, :, :, lanes(x)]
+    lax.fori_loop(4, 8, g1_own, 0)
+    wait(pending[1:])
+    lax.fori_loop(4, 8, g1_pair, 0)
+    pending_y = [send(g1_sum.at[high, p], g1_first_y.at[y], at_plane((x, p))) for p in ring_peers(y)]
+    g1_first_y[y] = g1_sum[4:8, y]
+
     bias_one_sum = jnp.sum(slope_one[...].astype(F32), axis=0, keepdims=True)
     for i in range(4):
         bias_mine[i : i + 1, :] = bias_one_sum[:, i * 128 : (i + 1) * 128]
         bias_mine[4 + i : 5 + i, :] = bias_two_sum[:, i * 128 : (i + 1) * 128]
     pending_bias = [send(bias_mine, bias_core, sibling)]
-
-    def g1_own(t, carry):
-        g1_keep[t] = dot_tn(own_in[:, lanes(2 * t + core)], slope_one[...])
-        return carry
-
-    lax.fori_loop(0, 8, g1_own, 0)
-    wait(pending_bias)
-    bias_pair[...] = bias_mine[...] + bias_core[...]
-    wait(pending)
-
-    def g1_pair(t, carry):
-        both = g1_keep[t] + g1_core[t].astype(F32)
-        g1_sum[t] = both.astype(BF16).reshape(4, 32, HID)
-        return carry
-
-    lax.fori_loop(0, 8, g1_pair, 0)
-
-    pending = [
-        send(g1_sum.at[:, p[1], :, lanes(p[0])], g1_plane.at[chip], at_plane(p)) for p in plane_peers
-    ]
-    pending_bias = [send(bias_pair, bias_plane.at[chip], at_plane(p)) for p in plane_peers]
-    g1_plane[chip] = g1_sum[:, y, :, lanes(x)]
-    bias_plane[chip] = bias_pair[...]
 
     wait(pending_g2)
     total = tree_sum([g2_plane[p].astype(F32) for p in range(16)])
@@ -364,16 +433,47 @@
     total = tree_sum([g2_z[p].astype(F32) for p in range(Z)])
     g2_row[rows(z, 16), :] = total.astype(BF16)
     pending_g2 = [send(g2_row.at[rows(z, 16), :], g2_row.at[rows(z, 16), :], at_z(p)) for p in z_peers]
+    wait(pending_bias)
+    bias_pair[...] = bias_mine[...] + bias_core[...]
+    pending_bias = [send(bias_pair, bias_x.at[x], at_plane((p, y))) for p in ring_peers(x)]
+    bias_x[x] = bias_pair[...]
+
+    wait(pending_x)
+
+    def g1_over_x(t, carry):
+        total = tree_sum([g1_first_x[p, t].astype(F32) for p in range(4)])
+        g1_part_x[t] = total.astype(BF16)
+        return carry
+
+    lax.fori_loop(0, 4, g1_over_x, 0)
+    pending_x = [send(g1_part_x.at[:, p], g1_then_y.at[y], at_plane((x, p))) for p in ring_peers(y)]
+    g1_then_y[y] = g1_part_x[:, y]
+    wait(pending_y)
+
+    def g1_over_y(t, carry):
+        total = tree_sum([g1_first_y[p, t].astype(F32) for p in range(4)])
+        g1_part_y[t] = total.astype(BF16)
+        return carry
+
+    lax.fori_loop(0, 4, g1_over_y, 0)
+    pending_y = [
+        send(g1_part_y.at[:, :, lanes(p)], g1_then_x.at[x], at_plane((p, y))) for p in ring_peers(x)
+    ]
+    g1_then_x[x] = g1_part_y[:, :, lanes(x)]
+    wait(pending_bias)
+    bias_row[...] = tree_sum([bias_x[p] for p in range(4)])
+    pending_bias = [send(bias_row, bias_y.at[y], at_plane((x, p))) for p in ring_peers(y)]
+    bias_y[y] = bias_row[...]
     wait(pending_g2)
-
-    wait(pending)
+    wait(pending_x)
+    wait(pending_y)
 
     def g1_chips(t, carry):
-        total = tree_sum([g1_plane[p, t].astype(F32) for p in range(16)])
-        g1_piece[t] = total.astype(BF16)
-        return carry
-
-    lax.fori_loop(0, 8, g1_chips, 0)
+        g1_piece[t] = tree_sum([g1_then_y[p, t].astype(F32) for p in range(4)]).astype(BF16)
+        g1_piece[4 + t] = tree_sum([g1_then_x[p, t].astype(F32) for p in range(4)]).astype(BF16)
+        return carry
+
+    lax.fori_loop(0, 4, g1_chips, 0)
     pending = [send(g1_piece.at[p], g1_z.at[z], at_z(p)) for p in z_peers]
     g1_z[z] = g1_piece[z]
     pending_g2 = [
@@ -381,7 +481,7 @@
     ]
     out_two[core, rows(y, 128), lanes(x)] = g2_row[...]
     wait(pending_bias)
-    bias_chips[...] = tree_sum([bias_plane[p] for p in range(16)])
+    bias_chips[...] = tree_sum([bias_y[p] for p in range(4)])
     pending_bias = [send(bias_chips, bias_z.at[z], at_z(p)) for p in z_peers]
     bias_z[z] = bias_chips[...]
     wait(pending)
@@ -403,6 +503,17 @@
 
 def training_step(*operands):
     bf16 = [
+        (SOURCES, COLS),
+        jnp.int32,
+        None,
+        (HID, HID),
+        (HID, HID),
+        None,
+        (OWN_SEEDS, HID),
+        jnp.int32,
+        jnp.int32,
+        None,
+        None,
         None,
         None,
         (Z - 1, OWN, COLS),
@@ -434,15 +545,42 @@
         (Z, 128, HID),
         (Z, 128, HID),
         (Z, 4, 32, HID),
-        (16, Z, 32, 128),
+        (4, 4, 4, 32, 128),
+        (4, 4, 32, 128),
+        (4, 4, 32, 128),
+        (4, 4, 32, HID),
+        (4, 32, HID),
+        (4, 4, 32, 128),
         (Z, 32, 128),
         (Z, 32, 128),
     ]
-    wide = iter([(SOURCES + 8, COLS), (OWN, COLS), (OWN_SEEDS, HID), (HID, HID), (Z, 128, HID)])
-    scratch = [pltpu.VMEM(s, BF16) if s else pltpu.VMEM(next(wide), F32) for s in bf16]
+    wide = iter(
+        [
+            (1, HID),
+            (1, HID),
+            (MIDDLE, 128),
+            (SEEDS, 128),
+            (SOURCES + 8, COLS),
+            (OWN, COLS),
+            (OWN_SEEDS, HID),
+            (HID, HID),
+            (Z, 128, HID),
+        ]
+    )
+    whole = iter([(16, 128), (FAN_TWO, SEEDS), (1, SEEDS)])
+    scratch = []
+    for entry in bf16:
+        if entry is None:
+            scratch.append(pltpu.VMEM(next(wide), F32))
+        elif entry is jnp.int32:
+            scratch.append(pltpu.VMEM(next(whole), jnp.int32))
+        else:
+            scratch.append(pltpu.VMEM(entry, BF16))
     tile = (8, 128)
-    scratch += [pltpu.VMEM(s, F32) for s in (tile, tile, tile, (16, *tile), tile, (Z, *tile))]
+    four = (4, *tile)
+    scratch += [pltpu.VMEM(s, F32) for s in (tile, tile, tile, four, tile, four, tile, (Z, *tile))]
     scratch += [pltpu.SemaphoreType.DMA((N_COPIES,)), pltpu.SemaphoreType.DMA((N_COPIES,))]
+    scratch += [pltpu.SemaphoreType.DMA((14,))]
     return pl.pallas_call(
         step_kernel,
         name="training_step",
@@ -451,11 +589,11 @@
             jax.ShapeDtypeStruct((2, HID, HID), BF16),
             jax.ShapeDtypeStruct(tile, F32),
         ),
-        in_specs=[SMEM, SMEM] + [VMEM] * (len(operands) - 2),
+        in_specs=[SMEM] + [HBM] * (len(operands) - 1),
         out_specs=(VMEM, VMEM, VMEM),
         scratch_shapes=scratch,
         compiler_params=pltpu.CompilerParams(
-            collective_id=0, has_side_effects=True, vmem_limit_bytes=48 << 20
+            collective_id=0, has_side_effects=True, vmem_limit_bytes=60 << 20
         ),
     )(*operands)
 
@@ -476,13 +614,10 @@
 ):
     slot = lax.broadcasted_iota(jnp.int32, nbr_one.shape, 0)
     index_one = jnp.where(slot < count_one[None, :], nbr_one, SOURCES).reshape(-1)
-    slot = lax.broadcasted_iota(jnp.int32, nbr_two.shape, 0)
-    index_two = jnp.where(slot < count_two[None, :], nbr_two, -1)
-    inverse_two = jnp.broadcast_to(1.0 / count_two.astype(F32)[:, None], (SEEDS, 128))
     one, two, bias = training_step(
         index_one,
-        1.0 / count_one.astype(F32),
         features,
+        count_one.reshape(MIDDLE // 128, 128),
         self_one,
         neigh_one,
         bias_one[None, :],
@@ -490,8 +625,8 @@
         neigh_two,
         bias_two[None, :],
         cotangent,
-        index_two,
-        inverse_two,
+        nbr_two,
+        count_two[None, :],
     )
     one, two = one.astype(F32), two.astype(F32)
     return one[0], one[1], bias[:4].reshape(HID), two[0], two[1], bias[4:].reshape(HID)

time: 122 us -> 105 us (0.86)
  Pallas kernels: 106 us -> 98.3 us
  local copies, waits for them, and re-layouts: 10.7 us -> 3.58 us
    pallas_call x1, Pallas kernels: 106 us -> 98.3 us  [training_step(): pl.pallas_call(step_kernel, name='training_step', out_shape=(jax.ShapeDty...]
    unnamed x16 -> x4, local copies, waits for them, and re-layouts: 7.69 us -> 0.01 us
    div x2 -> x0, other arithmetic: 1.39 us -> none  [the longest x1 0.7 us: on_device(): 1.0 / count_one.astype(F32)]
    convert_element_type x2, other arithmetic: 0.32 us -> 1.55 us  [on_device(): one, two = (one.astype(F32), two.astype(F32))]
where the time goes in v3:
time: 105 us
  Pallas kernels  98.3 us (94%)
  local copies, waits for them, and re-layouts  3.58 us (3%)
  other arithmetic  2.47 us (2%)
    pallas_call x1, Pallas kernels, training_step(): pl.pallas_call(step_kernel, name='training_step', out_shape=(jax.ShapeDty...  98.3 us

profile of v3, /device:TPU:1, one launch (start us, length us, event | category | flops | bytes accessed | tf_op | source)
XLA Modules:
  0.0 105.0 jit_solution(14127544639267943457)
XLA Ops:
  0.6 0.9 fusion
  1.6 0.7 reshape.25.index_one
  2.2 98.3 %training_step.1 = (bf16[2,128,512]{2,1,0:T(8,128)(2,1)}, bf16[2,512,512]{2,1,0:T(8,128)(2,1)}, f32[8,128]{1,0:T(8,128)}) custom-call(s32[30720]{0:T(1024)} %reshape.25.index_one, bf16[8192,128]{1,0:T(8,128)(2,1)} %features_in.1, s32[16,128]{1,0:T(8,128)} %bitcast.16, bf16[128,512]{1,0:T(8,128)(2,1)} %self_one.1, bf16[128,512]{1,0:T(8,128)(2,1)} %neigh_one.1, ...), custom_call_target="tpu_custom_call" | custom-call | tf_op jit(solution)/shard_map/training_step/pallas_call | solution.py:584
  100.5 1.5 %convert_element_type.7 = f32[2,512,512]{2,1,0:T(8,128)S(1)} convert(bf16[2,512,512]{2,1,0:T(8,128)(2,1)} %get-tuple-element.11) | non-fusion elementwise | flops 524288 | bytes 3145728 | tf_op jit(solution)/shard_map/convert_element_type | solution.py:631
  102.0 0.0 copy-start
  102.0 0.0 copy-start.1
  102.0 1.5 %slice_bitcast_fusion = (f32[512,512]{1,0:T(8,128)}, f32[512,512]{1,0:T(8,128)}) fusion(f32[2,512,512]{2,1,0:T(8,128)S(1)} %convert_element_type.7), kind=kLoop, calls=%fused_computation | loop fusion | bytes 4194304 | tf_op jit(solution)/shard_map/squeeze | solution.py:632
  103.5 0.0 copy-done
  103.6 0.8 slice_bitcast_fusion.2
  104.4 0.0 copy-done.1
  104.4 0.6 slice_bitcast_fusion.4
  (1 shorter events, 0.0 us)
Async XLA Ops:
  102.0 1.5 %copy-start = (bf16[2,128,512]{2,1,0:T(8,128)(2,1)S(1)}, bf16[2,128,512]{2,1,0:T(8,128)(2,1)}, u32[]{:S(2)}) copy-start(bf16[2,128,512]{2,1,0:T(8,128)(2,1)} %get-tuple-element.9) | copy-start | bytes 786436
  102.0 2.4 %copy-start.1 = (f32[8,128]{1,0:T(8,128)S(1)}, f32[8,128]{1,0:T(8,128)}, u32[]{:S(2)}) copy-start(f32[8,128]{1,0:T(8,128)} %get-tuple-element.10) | copy-start | bytes 12292

commit v4 on v3

--- a/solution.py
+++ b/solution.py
@@ -11,7 +11,6 @@
 F32 = jnp.float32
 BF16 = jnp.bfloat16
 VMEM = pl.BlockSpec(memory_space=pltpu.VMEM)
-SMEM = pl.BlockSpec(memory_space=pltpu.SMEM)
 HBM = pl.BlockSpec(memory_space=pltpu.HBM)
 
 SOURCES = 8192
@@ -51,7 +50,7 @@
 
 
 def step_kernel(
-    index_one,
+    index_one_in,
     features_in,
     count_one_in,
     self_one,
@@ -63,9 +62,16 @@
     cotangent_in,
     nbr_two_in,
     count_two_in,
+    result_self_one,
+    result_neigh_one,
+    result_self_two,
+    result_neigh_two,
+    result_bias_one,
+    result_bias_two,
+    index_one,
     out_one,
     out_two,
-    out_bias,
+    own_in_t,
     features,
     count_one,
     bias_one,
@@ -199,6 +205,7 @@
         (cotangent_in, cotangent),
         (nbr_two_in, nbr_two),
         (count_two_in, count_two),
+        (index_one_in, index_one),
     )
     loads += [
         pltpu.make_async_copy(src, dst, load_sem.at[4 + i]) for i, (src, dst) in enumerate(pairs)
@@ -213,12 +220,18 @@
 
     table[pl.ds(SOURCES, 8), :] = jnp.zeros((8, COLS), F32)
     steps = quarter // 256
-    loads[0].wait()
-    lax.fori_loop(0, steps, widen, 0)
+    for i in range(4):
+        loads[i].wait()
+        lax.fori_loop(i * steps, (i + 1) * steps, widen, 0)
     own_in[pl.ds(0, OWN_SEEDS), lanes(2 * z)] = features[rows(z, OWN_SEEDS), :]
     own_in[pl.ds(OWN_SEEDS, REST), lanes(2 * z)] = features[rows(z, REST, SEEDS), :]
     for load in loads[4:]:
         load.wait()
+
+    for i in range(MIDDLE // 128):
+        line = 1.0 / count_one[i : i + 1, :].astype(F32)
+        inverse_one[i * 128 : (i + 1) * 128, :] = jnp.broadcast_to(line, (128, 128)).T
+
     cols_mine = pl.ds(pl.multiple_of(core * 256, 256), 256)
     weights_one[z, rows(chip, 16), cols_mine] = weights_mine[rows(chip, 16), cols_mine]
     pl.semaphore_wait(barrier, len(everyone))
@@ -237,14 +250,6 @@
                 at_z(p),
             )
         )
-
-    for i in range(1, 4):
-        loads[i].wait()
-        lax.fori_loop(i * steps, (i + 1) * steps, widen, 0)
-
-    for i in range(MIDDLE // 128):
-        line = 1.0 / count_one[i : i + 1, :].astype(F32)
-        inverse_one[i * 128 : (i + 1) * 128, :] = jnp.broadcast_to(line, (128, 128)).T
 
     for turn, d in enumerate((4, 3, 5, 2, 6, 1, 7, 0)):
         owner = (z + d) % Z
@@ -280,17 +285,18 @@
     wait(pending_weights)
     wait(pending_own)
 
-    def layer_one(n, carry):
-        cols = pl.ds(pl.multiple_of(n * 256, 256), 256)
-        pre = dot(own_in[...], weights_one[:, :, cols].reshape(2 * Z * COLS, 256)) + bias_one[:, cols]
+    def layer_one(d, carry):
+        cols = lanes((col + d) % 4)
+        pre = dot(own_in[...], weights_one[:, :, cols].reshape(2 * Z * COLS, 128)) + bias_one[:, cols]
         act_own[:, cols] = jax.nn.softplus(pre).astype(BF16)
         return carry
 
-    lax.fori_loop(0, 2, layer_one, 0)
-
-    pending = [
-        send(act_own.at[:, lanes(p)], act_cols.at[rows(col, OWN), :], at_z(half * 4 + p)) for p in half_peers
-    ]
+    pending = []
+    for d in (2, 1, 3):
+        lax.fori_loop(d, d + 1, layer_one, 0)
+        p = (col + d) % 4
+        pending.append(send(act_own.at[:, lanes(p)], act_cols.at[rows(col, OWN), :], at_z(half * 4 + p)))
+    lax.fori_loop(0, 1, layer_one, 0)
     act_cols[rows(col, OWN), :] = act_own[:, lanes(col)]
 
     index_two = [
@@ -317,6 +323,12 @@
     pending = [send(mean_send.at[rows(p, OWN_SEEDS), :], mean_land.at[z], at_z(p)) for p in z_peers]
     mean_land[z] = mean_send[rows(z, OWN_SEEDS), :]
     pre_self = dot(act_own[pl.ds(0, OWN_SEEDS), :], self_two[...]) + bias_two[...]
+
+    def turn_block(t, carry):
+        own_in_t[rows(t, 128), :] = own_in[:, lanes(t)].T
+        return carry
+
+    lax.fori_loop(0, 2 * Z, turn_block, 0)
     wait(pending)
     for q in range(4):
         both = mean_land[q].astype(F32) + mean_land[4 + q].astype(F32)
@@ -354,15 +366,18 @@
     bias_two_sum = jnp.sum(slope_two[...].astype(F32), axis=0, keepdims=True)
     wait(pending)
 
-    def scatter_block(i, carry):
-        block = rows(i, OWN)
+    def scatter_block(d, carry):
+        block = rows((col + d) % 4, OWN)
         scat_send[block, :] = dot(counts[block, :], spread_cols[...]).astype(BF16)
         return carry
 
-    lax.fori_loop(0, 4, scatter_block, 0)
-    pending = [
-        send(scat_send.at[rows(p, OWN), :], scat_own.at[:, lanes(col)], at_z(half * 4 + p)) for p in half_peers
-    ]
+    pending = []
+    for first in (2, 0):
+        lax.fori_loop(first, first + 2, scatter_block, 0)
+        for d in (2, 3) if first else (1,):
+            p = (col + d) % 4
+            part = scat_send.at[rows(p, OWN), :]
+            pending.append(send(part, scat_own.at[:, lanes(col)], at_z(half * 4 + p)))
     scat_own[:, lanes(col)] = scat_send[rows(col, OWN), :]
     wait(pending_g2)
 
@@ -386,7 +401,7 @@
     slope_one[pl.ds(OWN_SEEDS, REST), :] = (back * gate).astype(BF16)
 
     def g1_block(t, carry):
-        g1_send[t] = dot_tn(own_in[:, lanes(2 * t + other)], slope_one[...]).astype(BF16)
+        g1_send[t] = dot(own_in_t[rows(2 * t + other, 128), :], slope_one[...]).astype(BF16)
         return carry
 
     pending = []
@@ -396,7 +411,7 @@
         pending.append(send(g1_send.at[chunk], g1_core.at[chunk], sibling))
 
     def g1_own(t, carry):
-        g1_keep[t] = dot_tn(own_in[:, lanes(2 * t + core)], slope_one[...])
+        g1_keep[t] = dot(own_in_t[rows(2 * t + core, 128), :], slope_one[...])
         return carry
 
     def g1_pair(t, carry):
@@ -493,16 +508,34 @@
     wait(pending_g2)
     pending_g2 = [send(out_two.at[core], out_two.at[core], sibling)]
     wait(pending_bias)
-    out_bias[...] = tree_sum([bias_z[p] for p in range(Z)])
+    total = tree_sum([bias_z[p] for p in range(Z)])
+    for i in range(4):
+        result_bias_one[:, i * 128 : (i + 1) * 128] = total[i : i + 1, :]
+        result_bias_two[:, i * 128 : (i + 1) * 128] = total[4 + i : 5 + i, :]
     wait(pending)
     pending = [send(out_one.at[core], out_one.at[core], sibling)]
     wait(pending_g2)
+    stores = [
+        pltpu.make_async_copy(out_two.at[0], result_self_two, load_sem.at[0]),
+        pltpu.make_async_copy(out_two.at[1], result_neigh_two, load_sem.at[1]),
+        pltpu.make_async_copy(out_one.at[0], result_self_one, load_sem.at[2]),
+        pltpu.make_async_copy(out_one.at[1], result_neigh_one, load_sem.at[3]),
+    ]
+    stores[0].start()
+    stores[1].start()
     wait(pending)
+    stores[2].start()
+    stores[3].start()
+    for store in stores:
+        store.wait()
     assert len(used) <= N_COPIES
 
 
 def training_step(*operands):
     bf16 = [
+        (2, 128, HID),
+        (2, HID, HID),
+        (2 * Z * COLS, OWN),
         (SOURCES, COLS),
         jnp.int32,
         None,
@@ -568,7 +601,7 @@
         ]
     )
     whole = iter([(16, 128), (FAN_TWO, SEEDS), (1, SEEDS)])
-    scratch = []
+    scratch = [pltpu.SMEM((FAN_ONE * MIDDLE,), jnp.int32)]
     for entry in bf16:
         if entry is None:
             scratch.append(pltpu.VMEM(next(wide), F32))
@@ -580,22 +613,50 @@
     four = (4, *tile)
     scratch += [pltpu.VMEM(s, F32) for s in (tile, tile, tile, four, tile, four, tile, (Z, *tile))]
     scratch += [pltpu.SemaphoreType.DMA((N_COPIES,)), pltpu.SemaphoreType.DMA((N_COPIES,))]
-    scratch += [pltpu.SemaphoreType.DMA((14,))]
+    scratch += [pltpu.SemaphoreType.DMA((15,))]
     return pl.pallas_call(
         step_kernel,
         name="training_step",
         out_shape=(
-            jax.ShapeDtypeStruct((2, 128, HID), BF16),
-            jax.ShapeDtypeStruct((2, HID, HID), BF16),
-            jax.ShapeDtypeStruct(tile, F32),
+            jax.ShapeDtypeStruct((128, HID), BF16),
+            jax.ShapeDtypeStruct((128, HID), BF16),
+            jax.ShapeDtypeStruct((HID, HID), BF16),
+            jax.ShapeDtypeStruct((HID, HID), BF16),
+            jax.ShapeDtypeStruct((1, HID), F32),
+            jax.ShapeDtypeStruct((1, HID), F32),
         ),
-        in_specs=[SMEM] + [HBM] * (len(operands) - 1),
-        out_specs=(VMEM, VMEM, VMEM),
+        in_specs=[HBM] * len(operands),
+        out_specs=(HBM, HBM, HBM, HBM, VMEM, VMEM),
         scratch_shapes=scratch,
         compiler_params=pltpu.CompilerParams(
             collective_id=0, has_side_effects=True, vmem_limit_bytes=60 << 20
         ),
     )(*operands)
+
+
+def widen_kernel(*refs):
+    half = len(refs) // 2
+    for narrow, wide in zip(refs[:half], refs[half:]):
+        wide[...] = narrow[...].astype(F32)
+
+
+def widen_all(*arrays):
+    steps = 2
+    specs = [
+        pl.BlockSpec((a.shape[0] // steps, HID), lambda i: (i, 0))
+        if a.shape[0] > 1
+        else pl.BlockSpec((1, HID), lambda i: (0, 0))
+        for a in arrays
+    ]
+    return pl.pallas_call(
+        widen_kernel,
+        name="widen",
+        grid=(steps,),
+        out_shape=[jax.ShapeDtypeStruct(a.shape, F32) for a in arrays],
+        in_specs=specs,
+        out_specs=specs,
+        compiler_params=pltpu.CompilerParams(vmem_limit_bytes=60 << 20),
+    )(*arrays)
 
 
 def on_device(
@@ -614,7 +675,7 @@
 ):
     slot = lax.broadcasted_iota(jnp.int32, nbr_one.shape, 0)
     index_one = jnp.where(slot < count_one[None, :], nbr_one, SOURCES).reshape(-1)
-    one, two, bias = training_step(
+    sums = training_step(
         index_one,
         features,
         count_one.reshape(MIDDLE // 128, 128),
@@ -628,8 +689,15 @@
         nbr_two,
         count_two[None, :],
     )
-    one, two = one.astype(F32), two.astype(F32)
-    return one[0], one[1], bias[:4].reshape(HID), two[0], two[1], bias[4:].reshape(HID)
+    g_self_one, g_neigh_one, g_self_two, g_neigh_two, g_bias_one, g_bias_two = widen_all(*sums)
+    return (
+        g_self_one,
+        g_neigh_one,
+        g_bias_one.reshape(HID),
+        g_self_two,
+        g_neigh_two,
+        g_bias_two.reshape(HID),
+    )
 
 
 def solution(mesh):

time: 105 us -> 99.5 us (0.948)
  local copies, waits for them, and re-layouts: 3.58 us -> 0.68 us
  other arithmetic: 2.47 us -> 0.92 us
  Pallas kernels: 98.3 us -> 97.1 us
    pallas_call x1, Pallas kernels: 98.3 us -> 94.4 us  [training_step(): pl.pallas_call(step_kernel, name='training_step', out_shape=(jax.ShapeDty...]
    pallas_call x0 -> x1, Pallas kernels: none -> 2.68 us  [widen_all(): pl.pallas_call(widen_kernel, name='widen', grid=(steps,), out_shape=[jax....]
    squeeze x2 -> x0, local copies, waits for them, and re-layouts: 2.31 us -> none  [the longest x1 1.49 us: on_device(): two[1]]
    convert_element_type x2 -> x0, other arithmetic: 1.55 us -> none  [on_device(): one, two = (one.astype(F32), two.astype(F32))]
where the time goes in v4:
time: 99.5 us; the launch traced here: 99.3 us
  Pallas kernels  97.1 us (98%)
    pallas_call x1, Pallas kernels, training_step(): pl.pallas_call(step_kernel, name='training_step', out_shape=(jax.ShapeDty...  94.4 us
    pallas_call x1, Pallas kernels, widen_all(): pl.pallas_call(widen_kernel, name='widen', grid=(steps,), out_shape=[jax....  2.68 us

profile of v4, /device:TPU:1, one launch (start us, length us, event | category | flops | bytes accessed | tf_op | source)
XLA Modules:
  0.0 99.3 jit_solution(5837704868947603504)
XLA Ops:
  0.6 0.9 fusion
  1.6 0.7 reshape.25.index_one_in
  2.2 94.4 %training_step.1 = (bf16[128,512]{1,0:T(8,128)(2,1)}, bf16[128,512]{1,0:T(8,128)(2,1)}, bf16[512,512]{1,0:T(8,128)(2,1)}, bf16[512,512]{1,0:T(8,128)(2,1)}, f32[1,512]{1,0:T(1,128)}, /*index=5*/f32[1,512]{1,0:T(1,128)}) custom-call(s32[30720]{0:T(1024)} %reshape.25.index_one_in, bf16[8192,128]{1,0:T(8,128)(2,1)} %features_in.1, s32[16,128]{1,0:T(8,128)} %bitcast.6, ...), custom_call_target="tpu_custom_call" | custom-call | tf_op jit(solution)/shard_map/training_step/pallas_call | solution.py:617
  96.7 2.7 %widen.1 = (f32[128,512]{1,0:T(8,128)}, f32[128,512]{1,0:T(8,128)}, f32[512,512]{1,0:T(8,128)}, f32[512,512]{1,0:T(8,128)}, f32[1,512]{1,0:T(1,128)}, /*index=5*/f32[1,512]{1,0:T(1,128)}) custom-call(bf16[128,512]{1,0:T(8,128)(2,1)} %get-tuple-element.18.refs_0_, bf16[128,512]{1,0:T(8,128)(2,1)} %get-tuple-element.19.refs_1_, ...), custom_call_target="tpu_custom_call" | custom-call | tf_op jit(solution)/shard_map/widen/pallas_call | solution.py:651

commit v5 on v4

--- a/solution.py
+++ b/solution.py
@@ -50,7 +50,7 @@
 
 
 def step_kernel(
-    index_one_in,
+    nbr_one_in,
     features_in,
     count_one_in,
     self_one,
@@ -69,6 +69,8 @@
     result_bias_one,
     result_bias_two,
     index_one,
+    masked,
+    nbr_one,
     out_one,
     out_two,
     own_in_t,
@@ -144,7 +146,7 @@
     chip = y * 4 + x
     other = 1 - core
     sibling = {"batch": b + 1 - 2 * core, "feat": z}
-    z_peers = [(z + d) % Z for d in range(1, Z)]
+    z_peers = [(z + d) % Z for d in (4, 3, 5, 2, 6, 1, 7)]
     ring_peers = lambda place: [(place + d) % 4 for d in range(1, 4)]
     half_peers = [(col + d) % 4 for d in range(1, 4)]
     plane_peers = [((x + d % 4) % 4, (y + d // 4) % 4) for d in range(1, 16)]
@@ -205,13 +207,34 @@
         (cotangent_in, cotangent),
         (nbr_two_in, nbr_two),
         (count_two_in, count_two),
-        (index_one_in, index_one),
+        (nbr_one_in, nbr_one),
     )
     loads += [
         pltpu.make_async_copy(src, dst, load_sem.at[4 + i]) for i, (src, dst) in enumerate(pairs)
     ]
     for load in loads:
         load.start()
+
+    loads[4].wait()
+    loads[5].wait()
+    cols_mine = pl.ds(pl.multiple_of(core * 256, 256), 256)
+    weights_one[z, rows(chip, 16), cols_mine] = weights_mine[rows(chip, 16), cols_mine]
+    pl.semaphore_wait(barrier, len(everyone))
+
+    part = weights_one.at[z, rows(chip, 16), cols_mine]
+    pending_weights = [send(weights_mine.at[rows(chip, 16), cols_mine], part, at_z(p)) for p in z_peers]
+    pending_own = []
+    for p in z_peers:
+        pending_own.append(
+            send(features_in.at[rows(p, OWN_SEEDS), :], own_in.at[pl.ds(0, OWN_SEEDS), lanes(2 * z)], at_z(p))
+        )
+        pending_own.append(
+            send(
+                features_in.at[rows(p, REST, SEEDS), :],
+                own_in.at[pl.ds(OWN_SEEDS, REST), lanes(2 * z)],
+                at_z(p),
+            )
+        )
 
     def widen(i, carry):
         block = pl.ds(pl.multiple_of(i * 256, 256), 256)
@@ -225,31 +248,24 @@
         lax.fori_loop(i * steps, (i + 1) * steps, widen, 0)
     own_in[pl.ds(0, OWN_SEEDS), lanes(2 * z)] = features[rows(z, OWN_SEEDS), :]
     own_in[pl.ds(OWN_SEEDS, REST), lanes(2 * z)] = features[rows(z, REST, SEEDS), :]
-    for load in loads[4:]:
+    for load in loads[6:]:
         load.wait()
 
+    lists = []
+    for k in range(FAN_ONE):
+        masked[k] = jnp.where(count_one[...] > k, nbr_one[k : k + 1, :], SOURCES)
+        lists.append(pltpu.make_async_copy(masked.at[k, 0], index_one[k], load_sem.at[15 + k]))
+        lists[-1].start()
+
     for i in range(MIDDLE // 128):
-        line = 1.0 / count_one[i : i + 1, :].astype(F32)
+        line = 1.0 / count_one[:, i * 128 : (i + 1) * 128].astype(F32)
         inverse_one[i * 128 : (i + 1) * 128, :] = jnp.broadcast_to(line, (128, 128)).T
-
-    cols_mine = pl.ds(pl.multiple_of(core * 256, 256), 256)
-    weights_one[z, rows(chip, 16), cols_mine] = weights_mine[rows(chip, 16), cols_mine]
-    pl.semaphore_wait(barrier, len(everyone))
-
-    part = weights_one.at[z, rows(chip, 16), cols_mine]
-    pending_weights = [send(weights_mine.at[rows(chip, 16), cols_mine], part, at_z(p)) for p in z_peers]
-    pending_own = []
-    for p in z_peers:
-        pending_own.append(
-            send(features.at[rows(p, OWN_SEEDS), :], own_in.at[pl.ds(0, OWN_SEEDS), lanes(2 * z)], at_z(p))
-        )
-        pending_own.append(
-            send(
-                features.at[rows(p, REST, SEEDS), :],
-                own_in.at[pl.ds(OWN_SEEDS, REST), lanes(2 * z)],
-                at_z(p),
-            )
-        )
+    for copy in lists:
+        copy.wait()
+
+    wait(pending_weights)
+    part = weights_one.at[:, rows(chip, 16), cols_mine]
+    pending_weights = [send(part, part, at_plane(p)) for p in plane_peers]
 
     for turn, d in enumerate((4, 3, 5, 2, 6, 1, 7, 0)):
         owner = (z + d) % Z
@@ -260,7 +276,7 @@
             base = jnp.where(g < OWN_SEEDS // GROUP, seed_base, rest_base)
             out = pl.multiple_of(g * GROUP, GROUP)
             for j in range(GROUP):
-                terms = [table[pl.ds(index_one[base + (k * MIDDLE + j)], 1), :] for k in range(FAN_ONE)]
+                terms = [table[pl.ds(index_one[k][base + j], 1), :] for k in range(FAN_ONE)]
                 total_one[pl.ds(out + j, 1), :] = tree_sum(terms)
             return carry
 
@@ -274,11 +290,7 @@
         else:
             own_in[pl.ds(0, OWN_SEEDS), lanes(2 * z + 1)] = seeds.astype(BF16)
             own_in[pl.ds(OWN_SEEDS, REST), lanes(2 * z + 1)] = rest.astype(BF16)
-        if turn == 1:
-            wait(pending_weights)
-            part = weights_one.at[:, rows(chip, 16), cols_mine]
-            pending_weights = [send(part, part, at_plane(p)) for p in plane_peers]
-        if turn == 6:
+        if turn == 5:
             wait(pending_weights)
             part = weights_one.at[:, :, cols_mine]
             pending_weights = [send(part, part, sibling)]
@@ -480,6 +492,10 @@
     pending_bias = [send(bias_row, bias_y.at[y], at_plane((x, p))) for p in ring_peers(y)]
     bias_y[y] = bias_row[...]
     wait(pending_g2)
+    pending_g2 = [
+        send(g2_row, out_two.at[core, rows(y, 128), lanes(x)], at_plane(p)) for p in plane_peers
+    ]
+    out_two[core, rows(y, 128), lanes(x)] = g2_row[...]
     wait(pending_x)
     wait(pending_y)
 
@@ -491,10 +507,6 @@
     lax.fori_loop(0, 4, g1_chips, 0)
     pending = [send(g1_piece.at[p], g1_z.at[z], at_z(p)) for p in z_peers]
     g1_z[z] = g1_piece[z]
-    pending_g2 = [
-        send(g2_row, out_two.at[core, rows(y, 128), lanes(x)], at_plane(p)) for p in plane_peers
-    ]
-    out_two[core, rows(y, 128), lanes(x)] = g2_row[...]
     wait(pending_bias)
     bias_chips[...] = tree_sum([bias_y[p] for p in range(4)])
     pending_bias = [send(bias_chips, bias_z.at[z], at_z(p)) for p in z_peers]
@@ -533,6 +545,8 @@
 
 def training_step(*operands):
     bf16 = [
+        jnp.int32,
+        jnp.int32,
         (2, 128, HID),
         (2, HID, HID),
         (2 * Z * COLS, OWN),
@@ -600,8 +614,8 @@
             (Z, 128, HID),
         ]
     )
-    whole = iter([(16, 128), (FAN_TWO, SEEDS), (1, SEEDS)])
-    scratch = [pltpu.SMEM((FAN_ONE * MIDDLE,), jnp.int32)]
+    whole = iter([(FAN_ONE, 1, MIDDLE), (FAN_ONE, MIDDLE), (1, MIDDLE), (FAN_TWO, SEEDS), (1, SEEDS)])
+    scratch = [[pltpu.SMEM((MIDDLE,), jnp.int32) for k in range(FAN_ONE)]]
     for entry in bf16:
         if entry is None:
             scratch.append(pltpu.VMEM(next(wide), F32))
@@ -613,7 +627,7 @@
     four = (4, *tile)
     scratch += [pltpu.VMEM(s, F32) for s in (tile, tile, tile, four, tile, four, tile, (Z, *tile))]
     scratch += [pltpu.SemaphoreType.DMA((N_COPIES,)), pltpu.SemaphoreType.DMA((N_COPIES,))]
-    scratch += [pltpu.SemaphoreType.DMA((15,))]
+    scratch += [pltpu.SemaphoreType.DMA((15 + FAN_ONE,))]
     return pl.pallas_call(
         step_kernel,
         name="training_step",
@@ -673,12 +687,10 @@
     bias_two,
     cotangent,
 ):
-    slot = lax.broadcasted_iota(jnp.int32, nbr_one.shape, 0)
-    index_one = jnp.where(slot < count_one[None, :], nbr_one, SOURCES).reshape(-1)
     sums = training_step(
-        index_one,
+        nbr_one,
         features,
-        count_one.reshape(MIDDLE // 128, 128),
+        count_one[None, :],
         self_one,
         neigh_one,
         bias_one[None, :],

time: 99.5 us -> 97.5 us (0.980)
  no operation moved by 1% of the time
where the time goes in v5:
time: 97.5 us; the launch traced here: 97.4 us
  Pallas kernels  96.7 us (99%)
    pallas_call x1, Pallas kernels, training_step(): pl.pallas_call(step_kernel, name='training_step', out_shape=(jax.ShapeDty...  94 us
    pallas_call x1, Pallas kernels, widen_all(): pl.pallas_call(widen_kernel, name='widen', grid=(steps,), out_shape=[jax....  2.68 us

profile of v5, /device:TPU:1, one launch (start us, length us, event | category | flops | bytes accessed | tf_op | source)
XLA Modules:
  0.0 97.4 jit_solution(18320569554127982640)
XLA Ops:
  0.6 94.0 %training_step.1 = (bf16[128,512]{1,0:T(8,128)(2,1)}, bf16[128,512]{1,0:T(8,128)(2,1)}, bf16[512,512]{1,0:T(8,128)(2,1)}, bf16[512,512]{1,0:T(8,128)(2,1)}, f32[1,512]{1,0:T(1,128)}, /*index=5*/f32[1,512]{1,0:T(1,128)}) custom-call(s32[15,2048]{1,0:T(8,128)} %nbr_one_in.1, bf16[8192,128]{1,0:T(8,128)(2,1)} %features_in.1, s32[1,2048]{1,0:T(1,128)} %bitcast.6, ...), custom_call_target="tpu_custom_call" | custom-call | tf_op jit(solution)/shard_map/training_step/pallas_call | solution.py:631
  94.7 2.7 %widen.1 = (f32[128,512]{1,0:T(8,128)}, f32[128,512]{1,0:T(8,128)}, f32[512,512]{1,0:T(8,128)}, f32[512,512]{1,0:T(8,128)}, f32[1,512]{1,0:T(1,128)}, /*index=5*/f32[1,512]{1,0:T(1,128)}) custom-call(bf16[128,512]{1,0:T(8,128)(2,1)} %get-tuple-element.18.refs_0_, bf16[128,512]{1,0:T(8,128)(2,1)} %get-tuple-element.19.refs_1_, ...), custom_call_target="tpu_custom_call" | custom-call | tf_op jit(solution)/shard_map/widen/pallas_call | solution.py:665

commit v6 on v5

--- a/solution.py
+++ b/solution.py
@@ -236,6 +236,15 @@
             )
         )
 
+    loads[6].wait()
+    loads[14].wait()
+
+    lists = []
+    for k in range(FAN_ONE):
+        masked[k] = jnp.where(count_one[...] > k, nbr_one[k : k + 1, :], SOURCES)
+        lists.append(pltpu.make_async_copy(masked.at[k, 0], index_one[k], load_sem.at[15 + k]))
+        lists[-1].start()
+
     def widen(i, carry):
         block = pl.ds(pl.multiple_of(i * 256, 256), 256)
         table[block, :] = features[block, :].astype(F32)
@@ -248,15 +257,6 @@
         lax.fori_loop(i * steps, (i + 1) * steps, widen, 0)
     own_in[pl.ds(0, OWN_SEEDS), lanes(2 * z)] = features[rows(z, OWN_SEEDS), :]
     own_in[pl.ds(OWN_SEEDS, REST), lanes(2 * z)] = features[rows(z, REST, SEEDS), :]
-    for load in loads[6:]:
-        load.wait()
-
-    lists = []
-    for k in range(FAN_ONE):
-        masked[k] = jnp.where(count_one[...] > k, nbr_one[k : k + 1, :], SOURCES)
-        lists.append(pltpu.make_async_copy(masked.at[k, 0], index_one[k], load_sem.at[15 + k]))
-        lists[-1].start()
-
     for i in range(MIDDLE // 128):
         line = 1.0 / count_one[:, i * 128 : (i + 1) * 128].astype(F32)
         inverse_one[i * 128 : (i + 1) * 128, :] = jnp.broadcast_to(line, (128, 128)).T
@@ -294,6 +294,8 @@
             wait(pending_weights)
             part = weights_one.at[:, :, cols_mine]
             pending_weights = [send(part, part, sibling)]
+    for i in range(7, 14):
+        loads[i].wait()
     wait(pending_weights)
     wait(pending_own)
 
@@ -376,6 +378,18 @@
 
     lax.fori_loop(0, 2, direct_block, 0)
     bias_two_sum = jnp.sum(slope_two[...].astype(F32), axis=0, keepdims=True)
+    wait(pending_g2)
+
+    def g2_pair(i, carry):
+        block = rows(i, 128)
+        g2_sum[block, :] = (g2_keep[block, :] + g2_core[block, :].astype(F32)).astype(BF16)
+        return carry
+
+    lax.fori_loop(0, 4, g2_pair, 0)
+    pending_g2 = [
+        send(g2_sum.at[rows(p[1], 128), lanes(p[0])], g2_plane.at[chip], at_plane(p)) for p in plane_peers
+    ]
+    g2_plane[chip] = g2_sum[rows(y, 128), lanes(x)]
     wait(pending)
 
     def scatter_block(d, carry):
@@ -391,18 +405,6 @@
             part = scat_send.at[rows(p, OWN), :]
             pending.append(send(part, scat_own.at[:, lanes(col)], at_z(half * 4 + p)))
     scat_own[:, lanes(col)] = scat_send[rows(col, OWN), :]
-    wait(pending_g2)
-
-    def g2_pair(i, carry):
-        block = rows(i, 128)
-        g2_sum[block, :] = (g2_keep[block, :] + g2_core[block, :].astype(F32)).astype(BF16)
-        return carry
-
-    lax.fori_loop(0, 4, g2_pair, 0)
-    pending_g2 = [
-        send(g2_sum.at[rows(p[1], 128), lanes(p[0])], g2_plane.at[chip], at_plane(p)) for p in plane_peers
-    ]
-    g2_plane[chip] = g2_sum[rows(y, 128), lanes(x)]
     wait(pending)
 
     back = scat_own[pl.ds(0, OWN_SEEDS), :].astype(F32) + direct[...]

time: 97.5 us -> 97.2 us (level)
  no operation moved by 1% of the time
where the time goes in v6:
time: 97.2 us; the launch traced here: 97.1 us
  Pallas kernels  96.4 us (99%)
    pallas_call x1, Pallas kernels, training_step(): pl.pallas_call(step_kernel, name='training_step', out_shape=(jax.ShapeDty...  93.8 us
    pallas_call x1, Pallas kernels, widen_all(): pl.pallas_call(widen_kernel, name='widen', grid=(steps,), out_shape=[jax....  2.68 us

profile of v6, /device:TPU:1, one launch (start us, length us, event | category | flops | bytes accessed | tf_op | source)
XLA Modules:
  0.0 97.1 jit_solution(4375321911450998427)
XLA Ops:
  0.6 93.8 %training_step.1 = (bf16[128,512]{1,0:T(8,128)(2,1)}, bf16[128,512]{1,0:T(8,128)(2,1)}, bf16[512,512]{1,0:T(8,128)(2,1)}, bf16[512,512]{1,0:T(8,128)(2,1)}, f32[1,512]{1,0:T(1,128)}, /*index=5*/f32[1,512]{1,0:T(1,128)}) custom-call(s32[15,2048]{1,0:T(8,128)} %nbr_one_in.1, bf16[8192,128]{1,0:T(8,128)(2,1)} %features_in.1, s32[1,2048]{1,0:T(1,128)} %bitcast.6, ...), custom_call_target="tpu_custom_call" | custom-call | tf_op jit(solution)/shard_map/training_step/pallas_call | solution.py:633
  94.4 2.7 %widen.1 = (f32[128,512]{1,0:T(8,128)}, f32[128,512]{1,0:T(8,128)}, f32[512,512]{1,0:T(8,128)}, f32[512,512]{1,0:T(8,128)}, f32[1,512]{1,0:T(1,128)}, /*index=5*/f32[1,512]{1,0:T(1,128)}) custom-call(bf16[128,512]{1,0:T(8,128)(2,1)} %get-tuple-element.18.refs_0_, bf16[128,512]{1,0:T(8,128)(2,1)} %get-tuple-element.19.refs_1_, ...), custom_call_target="tpu_custom_call" | custom-call | tf_op jit(solution)/shard_map/widen/pallas_call | solution.py:667
